TPU v7x, 256 devices: a whole 4x4x8 slice. The times are simulated.
256 devices in a mesh: section: 8 (over z_lo, core), mesh: 32 (over x, z_hi, y).
Axes of the slice: x: 4, y: 4, z: 8 (z_hi: 2, z_lo: 4; z = z_hi * 4 + z_lo), core: 2. Of those that a mesh axis runs over, the one named last changes fastest.
Arguments:
- saved_inputs: bfloat16 [8, 3, 8192, 1024], P('section', None, 'mesh'), may hold values from -8 to 8
- w_query: bfloat16 [8, 1024, 1024], P('section'), may hold values from -6 to 6
- w_key: bfloat16 [8, 1024, 1024], P('section'), may hold values from -6 to 6
- w_value: bfloat16 [8, 1024, 1024], P('section'), may hold values from -0.1875 to 0.1875
- w_out: bfloat16 [8, 1024, 1024], P('section'), may hold values from -0.1875 to 0.1875
- pending: bfloat16 [8, 8192, 1024], P('section', 'mesh'), may hold values from -6 to 6
- top_grads: bfloat16 [1, 8192, 1024], P(None, 'mesh'), may hold values from -6 to 6
- key_blocks: int32 [64, 2], P('mesh'), may hold values from -1 to 63, as said below
- counts: int32 [64], replicated, may hold values from 64 to 128, as said below
- plan: int32 [2, 8], replicated, may hold values from 0 to 2
Outputs:
- layer_grads: float32 [8, 1024, 4, 1024], P('section', 'mesh')
- input_grads: bfloat16 [2, 8, 8192, 1024], P(None, 'section', 'mesh')
Inputs may be any that keep to these rules, and one draw needn't show every extreme that they name: `key_blocks`: entry j of block b is -1 (nothing read) or the block (b + o_j) modulo 64, with o = (1, -1). `counts`: the padding nodes of a block are its last ones.
All inputs are finite; a program needn't handle non-finite values.
Results may differ from a plain program's by a relative error of at most 0.03.
The roundings to bfloat16 on the way count: a program that leaves them out, or rounds other values in their place, can miss the bound.
Values may be sent and summed in bfloat16 or wider, within the bound.
No kernel may reach another device: no remote copies, remote signals or barrier semaphores. Data moves between devices by JAX's collectives and lax.ppermute only.
A program may use at most 128 MiB of HBM per device.

v0:
```python
import math

import jax
import jax.numpy as jnp
from jax import lax
from jax.sharding import PartitionSpec as P

HEADS = 8
BLOCK = 128


OFFSETS = (1, -1)
EPSILON = 1e-06


def from_behind(value, axis, steps):
    count = lax.axis_size(axis)
    pairs = [(source, (source + steps) % count) for source in range(count)]
    return lax.ppermute(value, axis, pairs)


def shifted(x, axis, by):
    size = lax.axis_size(axis)
    pairs = [(i, i + by) for i in range(size) if 0 <= i + by < size]
    return lax.ppermute(x, axis, pairs)


def right_dot(left, right):
    return lax.dot_general(
        left, right, (((1,), (1,)), ((), ())), preferred_element_type=jnp.float32
    )


def left_dot(left, right):
    return lax.dot_general(
        left, right, (((0,), (0,)), ((), ())), preferred_element_type=jnp.float32
    )


def weight_rows(terms, row_count):
    normed, grad_joined, attended, upstream = terms
    features = upstream.shape[1]
    projected = left_dot(normed, grad_joined).reshape(row_count, 3, features)
    return jnp.concatenate([projected, left_dot(attended, upstream)[:, None]], axis=1)


def per_device(
    saved_inputs, w_query, w_key, w_value, w_out, pending, top_grads, key_blocks, counts, plan
):
    sections = lax.axis_size("section")
    section_here = lax.axis_index("section")
    part_count = lax.axis_size("mesh")
    part_here = lax.axis_index("mesh")
    rows_here = pending.shape[1]
    features = pending.shape[2]
    block_rows = BLOCK
    blocks_here = rows_here // block_rows
    head_dim = features // HEADS
    tick_count = plan.shape[0]
    score_scale = 1.0 / math.sqrt(head_dim)
    slot_count = 1 + len(OFFSETS)
    query_weight = w_query[0]
    key_weight = w_key[0]
    value_weight = w_value[0]
    out_weight = w_out[0]
    positions = jnp.arange(block_rows)
    block_ids = jnp.arange(counts.shape[0])
    global_ids = part_here * blocks_here + jnp.arange(blocks_here)
    own_count = jnp.sum(
        jnp.where(block_ids[None, :] == global_ids[:, None], counts[None, :], 0), axis=1
    )
    listed_counts = jnp.sum(
        jnp.where(block_ids[None, None, :] == key_blocks[:, :, None], counts[None, None, :], 0),
        axis=2,
    )
    own_valid = positions[None, :] < own_count[:, None]
    listed_valid = positions[None, None, :] < listed_counts[:, :, None]
    key_valid = jnp.concatenate([own_valid[:, None, :], listed_valid], axis=1).reshape(
        blocks_here, slot_count * block_rows
    )
    member_ids = jnp.sum(jnp.where(jnp.arange(sections)[None, :] == section_here, plan, 0), axis=1)
    slot_offsets = (0,) + OFFSETS
    upstream = pending[0]
    outgoing = []
    layer_total = None
    for tick_index in range(tick_count):
        x_in = lax.dynamic_index_in_dim(saved_inputs[0], member_ids[tick_index], 0, keepdims=False)
        x_float = x_in.astype(jnp.float32)
        inv_rms = lax.rsqrt(jnp.mean(x_float * x_float, axis=-1, keepdims=True) + EPSILON)
        normed_float = x_float * inv_rms
        normed = normed_float.astype(jnp.bfloat16)
        queries = jnp.dot(normed, query_weight, preferred_element_type=jnp.float32).astype(
            jnp.bfloat16
        )
        key_rows = jnp.dot(normed, key_weight, preferred_element_type=jnp.float32).astype(
            jnp.bfloat16
        )
        value_rows = jnp.dot(normed, value_weight, preferred_element_type=jnp.float32).astype(
            jnp.bfloat16
        )
        own_pair = jnp.stack([key_rows, value_rows])
        edge_pairs = []
        for direction in (1, -1):
            edge_rows = (
                own_pair[:, rows_here - block_rows :]
                if direction == 1
                else own_pair[:, :block_rows]
            )
            edge_pairs.append(from_behind(edge_rows, "mesh", direction))
        extended = jnp.concatenate([edge_pairs[0], own_pair, edge_pairs[1]], axis=1)
        ext_blocks = extended.reshape(2, blocks_here + 2, block_rows, features)
        chosen = jnp.stack(
            [ext_blocks[:, 1 + offset : 1 + offset + blocks_here] for offset in slot_offsets],
            axis=2,
        )
        key_heads = chosen[0].reshape(blocks_here, slot_count * block_rows, HEADS, head_dim)
        value_heads = chosen[1].reshape(blocks_here, slot_count * block_rows, HEADS, head_dim)
        query_heads = queries.reshape(blocks_here, block_rows, HEADS, head_dim)
        scores = (
            jnp.einsum(
                "bqhd,bkhd->bhqk", query_heads, key_heads, preferred_element_type=jnp.float32
            )
            * score_scale
        )
        scores = jnp.where(key_valid[:, None, None, :], scores, -jnp.inf)
        peak = jnp.max(scores, axis=-1, keepdims=True)
        raised = jnp.exp(scores - peak)
        probs = raised / jnp.sum(raised, axis=-1, keepdims=True)
        probs_bf = probs.astype(jnp.bfloat16)
        attended = (
            jnp.einsum("bhqk,bkhd->bqhd", probs_bf, value_heads, preferred_element_type=jnp.float32)
            .reshape(rows_here, features)
            .astype(jnp.bfloat16)
        )
        grad_attended = right_dot(upstream, out_weight).astype(jnp.bfloat16)
        grad_heads = grad_attended.reshape(blocks_here, block_rows, HEADS, head_dim)
        grad_probs = jnp.einsum(
            "bqhd,bkhd->bhqk", grad_heads, value_heads, preferred_element_type=jnp.float32
        )
        grad_scores = (
            probs * (grad_probs - jnp.sum(probs * grad_probs, axis=-1, keepdims=True)) * score_scale
        )
        scores_bf = grad_scores.astype(jnp.bfloat16)
        grad_query = (
            jnp.einsum("bhqk,bkhd->bqhd", scores_bf, key_heads, preferred_element_type=jnp.float32)
            .reshape(rows_here, features)
            .astype(jnp.bfloat16)
        )
        key_terms = jnp.einsum(
            "bhqk,bqhd->bkhd", scores_bf, query_heads, preferred_element_type=jnp.float32
        ).reshape(blocks_here, slot_count, block_rows, features)
        value_terms = jnp.einsum(
            "bhqk,bqhd->bkhd", probs_bf, grad_heads, preferred_element_type=jnp.float32
        ).reshape(blocks_here, slot_count, block_rows, features)
        own_list = []
        before_list = []
        after_list = []
        for terms_now in (key_terms, value_terms):
            zero_block = jnp.zeros_like(terms_now[:1, 0])
            own_now = (
                terms_now[:, 0]
                + jnp.concatenate([zero_block, terms_now[:-1, 1]], axis=0)
                + jnp.concatenate([terms_now[1:, 2], zero_block], axis=0)
            )
            own_list.append(own_now)
            before_list.append(terms_now[0, 2])
            after_list.append(terms_now[blocks_here - 1, 1])
        own_terms = jnp.stack(own_list)
        for direction in (-1, 1):
            edge_terms = jnp.stack(before_list) if direction == -1 else jnp.stack(after_list)
            target_index = blocks_here - 1 if direction == -1 else 0
            returned = from_behind(edge_terms.astype(jnp.bfloat16), "mesh", direction)
            own_terms = own_terms.at[:, target_index].add(returned.astype(jnp.float32))
        grad_key = own_terms[0].reshape(rows_here, features).astype(jnp.bfloat16)
        grad_value = own_terms[1].reshape(rows_here, features).astype(jnp.bfloat16)
        grad_normed = (
            right_dot(grad_query, query_weight)
            + right_dot(grad_key, key_weight)
            + right_dot(grad_value, value_weight)
        )
        grad_input = inv_rms * (
            grad_normed
            - normed_float * jnp.mean(grad_normed * normed_float, axis=-1, keepdims=True)
        )
        grad_x = (upstream.astype(jnp.float32) + grad_input).astype(jnp.bfloat16)
        outgoing.append(grad_x)
        grad_joined = jnp.concatenate([grad_query, grad_key, grad_value], axis=1)
        terms = (normed, grad_joined, attended, upstream)

        def tick_rows(first_row, row_count, terms=terms):
            return weight_rows(terms, row_count)

        tick_sum = lax.psum_scatter(
            tick_rows(jnp.int32(0), features // part_count * lax.axis_size("mesh")).astype(
                jnp.bfloat16
            ),
            "mesh",
            scatter_dimension=0,
            tiled=True,
        ).astype(jnp.float32)
        layer_total = tick_sum if layer_total is None else layer_total + tick_sum
        if tick_index + 1 < tick_count:
            passed = shifted(grad_x, "section", -1)
            upstream = jnp.where(section_here == sections - 1, top_grads[tick_index], passed)
    return (layer_total[None], jnp.stack(outgoing)[:, None])


def solution(mesh):
    in_specs = (
        P("section", None, "mesh", None),
        P("section", None, None),
        P("section", None, None),
        P("section", None, None),
        P("section", None, None),
        P("section", "mesh", None),
        P(None, "mesh", None),
        P("mesh", None),
        P(),
        P(),
    )
    out_specs = (P("section", "mesh", None, None), P(None, "section", "mesh", None))
    return jax.shard_map(
        per_device, mesh=mesh, in_specs=in_specs, out_specs=out_specs, check_vma=False
    )
```

profile of v0, /device:TPU:32, one launch (start us, length us, event | category | flops | bytes accessed | tf_op | source)
XLA Modules:
  0.0 763.2 jit_solution(17673679516054231990)
XLA Ops:
  14.1 2.5 fusion.139
  21.5 9.4 %collective-permute-start.1 = (bf16[2,128,1024]{2,1,0:T(8,128)(2,1)}, bf16[2,128,1024]{2,1,0:T(8,128)(2,1)}, u32[]{:S(2)}, u32[]{:S(2)}) collective-permute-start(bf16[2,128,1024]{2,1,0:T(8,128)(2,1)} %get-tuple-element.91), channel_id=1, source_target_pairs={{0,31},{1,0},{2,1},{3,2},{4,3},{5,4},{6,5},{7,6},{8,7},{9,8},{10,9... | collective-permute-start | bytes 1572872 | tf_op jit(solution)/shard_map/ppermute | solution.py:19
  31.5 2.6 fusion.133
  35.3 2.3 fusion.127
  38.1 16.4 %collective-permute-done = bf16[2,128,1024]{2,1,0:T(8,128)(2,1)} collective-permute-done((bf16[2,128,1024]{2,1,0:T(8,128)(2,1)}, bf16[2,128,1024]{2,1,0:T(8,128)(2,1)}, u32[]{:S(2)}, u32[]{:S(2)}) %collective-permute-start) | collective-permute-done | bytes 524320 | tf_op jit(solution)/shard_map/ppermute | solution.py:19
  60.1 3.0 copy.98
  63.1 3.0 copy.128
  66.1 2.8 copy.88
  69.0 3.8 fusion.238
  72.7 4.1 fusion.236
  76.9 4.2 fusion.148
  81.1 2.3 convolution_bitcast_fusion.1
  83.4 17.9 %fusion.55 = f32[2,384,8,128]{1,3,2,0:T(8,128)} fusion(bf16[2,128,8,128]{1,3,2,0:T(8,128)(2,1)S(1)} %copy-done.35, f32[2,8,128,384]{3,2,1,0:T(8,128)} %fusion.238, f32[2,8,128,384]{3,2,1,0:T(8,128)} %get-tuple-element.95, f32[2,8,128]{2,1,0:T(8,128)S(1)} %get-tuple-element.94), kind=kOutput, calls=%fused_computation.65 | convolution fusion | flops 206834048 | bytes 9969664 | tf_op jit(solution)/shard_map/bhqk,bqhd->bkhd/dot_general | solution.py:149
  101.3 3.6 copy.91
  104.8 4.6 reshape.346
  109.5 2.3 slice_bitcast_fusion.17
  111.7 3.3 convert.60
  115.0 3.6 copy.94
  118.6 4.6 reshape.347
  124.4 2.1 convert.61
  128.6 5.3 collective-permute-start.2
  135.0 2.9 fusion.180
  138.0 17.2 %fusion.118 = bf16[2,128,8,128]{1,3,2,0:T(8,128)(2,1)} fusion(bf16[2,384,8,128]{1,3,2,0:T(8,128)(2,1)} %copy.88, f32[2,8,128,384]{3,2,1,0:T(8,128)} %fusion.238, f32[2,8,128,384]{3,2,1,0:T(8,128)} %get-tuple-element.95, f32[2,8,128]{2,1,0:T(8,128)S(1)} %get-tuple-element.94), kind=kOutput, calls=%fused_computation.110 | convolution fusion | flops 207096192 | bytes 8396800 | tf_op jit(solution)/shard_map/bhqk,bkhd->bqhd/dot_general | solution.py:145
  155.2 2.7 pad_maximum_fusion.4
  157.9 2.1 copy.89
  163.4 3.3 convert_bitcast_fusion.1
  171.4 2.6 copy.96
  174.0 6.4 convolution_convert_fusion.1
  180.4 6.8 pad_maximum_fusion
  187.3 2.5 fusion.136
  193.0 10.6 %collective-permute-start.5 = (bf16[2,128,1024]{2,1,0:T(8,128)(2,1)}, bf16[2,128,1024]{2,1,0:T(8,128)(2,1)}, u32[]{:S(2)}, u32[]{:S(2)}) collective-permute-start(bf16[2,128,1024]{2,1,0:T(8,128)(2,1)} %get-tuple-element.89), channel_id=1, source_target_pairs={{0,31},{1,0},{2,1},{3,2},{4,3},{5,4},{6,5},{7,6},{8,7},{9,8},{10,9... | collective-permute-start | bytes 1572872 | tf_op jit(solution)/shard_map/ppermute | solution.py:19
  203.6 2.6 fusion.130
  207.4 7.0 collective-permute-done.4
  214.4 20.1 %collective-permute-done.5 = bf16[2,128,1024]{2,1,0:T(8,128)(2,1)} collective-permute-done((bf16[2,128,1024]{2,1,0:T(8,128)(2,1)}, bf16[2,128,1024]{2,1,0:T(8,128)(2,1)}, u32[]{:S(2)}, u32[]{:S(2)}) %collective-permute-start.5) | collective-permute-done | bytes 524320 | tf_op jit(solution)/shard_map/ppermute | solution.py:19
  240.2 2.9 copy.106
  243.1 3.0 copy.138
  246.1 2.9 copy.116
  249.1 3.3 fusion.18
  252.4 4.4 fusion.237
  256.8 2.5 fusion.26
  260.7 2.2 collective-permute-start.6
  264.7 2.1 copy.117
  266.8 12.3 %collective-permute-done.6 = bf16[256,1024]{1,0:T(8,128)(2,1)} collective-permute-done((bf16[256,1024]{1,0:T(8,128)(2,1)S(1)}, bf16[256,1024]{1,0:T(8,128)(2,1)}, u32[]{:S(2)}, u32[]{:S(2)}) %collective-permute-start.6) | collective-permute-done | bytes 524320 | tf_op jit(solution)/shard_map/ppermute | solution.py:25
  280.2 2.5 fusion.124
  283.3 4.3 convolution_bitcast_fusion
  287.5 3.6 copy.112
  291.1 4.5 reshape.354
  295.7 3.7 fusion.239
  299.4 17.8 %fusion.52 = f32[2,384,8,128]{1,3,2,0:T(8,128)} fusion(bf16[2,128,8,128]{1,3,2,0:T(8,128)(2,1)S(1)} %copy-done.34, f32[2,8,128,384]{3,2,1,0:T(8,128)} %fusion.239, f32[2,8,128,384]{3,2,1,0:T(8,128)} %get-tuple-element.99, f32[2,8,128]{2,1,0:T(8,128)S(1)} %get-tuple-element.98), kind=kOutput, calls=%fused_computation.64 | convolution fusion | flops 206834048 | bytes 9969664 | tf_op jit(solution)/shard_map/bhqk,bqhd->bkhd/dot_general | solution.py:149
  317.2 3.6 copy.109
  320.8 4.5 reshape.353
  325.3 2.3 convert.66
  329.4 12.9 %collective-permute-start.7 = (bf16[2,128,1024]{2,1,0:T(8,128)(2,1)}, bf16[2,128,1024]{2,1,0:T(8,128)(2,1)}, u32[]{:S(2)}, u32[]{:S(2)}) collective-permute-start(bf16[2,128,1024]{2,1,0:T(8,128)(2,1)} %pad_maximum_fusion.12), channel_id=1, source_target_pairs={{0,31},{1,0},{2,1},{3,2},{4,3},{5,4},{6,5},{7,6},{8,7},{9,8},{10,9... | collective-permute-start | bytes 1572872 | tf_op jit(solution)/shard_map/ppermute | solution.py:19
  344.7 17.2 %fusion.121 = bf16[2,128,8,128]{1,3,2,0:T(8,128)(2,1)} fusion(bf16[2,384,8,128]{1,3,2,0:T(8,128)(2,1)} %copy.106, f32[2,8,128,384]{3,2,1,0:T(8,128)} %fusion.239, f32[2,8,128,384]{3,2,1,0:T(8,128)} %get-tuple-element.99, f32[2,8,128]{2,1,0:T(8,128)S(1)} %get-tuple-element.98), kind=kOutput, calls=%fused_computation.111 | convolution fusion | flops 207096192 | bytes 8396800 | tf_op jit(solution)/shard_map/bhqk,bkhd->bqhd/dot_general | solution.py:145
  366.1 2.1 copy.107
  369.5 3.4 convert_bitcast_fusion
  372.9 6.1 collective-permute-done.7
  380.2 5.9 collective-permute-done.8
  389.7 2.6 copy.114
  392.3 6.4 convolution_convert_fusion
  398.6 6.7 pad_maximum_fusion.1
  406.4 2.5 fusion.16
  413.4 72.6 %reduce-scatter.3.cloned.1.call-done = bf16[32,4,1024]{2,0,1:T(8,128)(2,1)} async-done(((bf16[1024,4,1024]{2,0,1:T(8,128)(2,1)}), bf16[32,4,1024]{2,0,1:T(8,128)(2,1)}) %reduce-scatter.3.cloned.1.call-update) | async-done | bytes 262160 | tf_op jit(solution)/shard_map/reduce_scatter | solution.py:193
  486.0 267.9 %reduce-scatter.5.cloned.1.call-done = bf16[32,4,1024]{2,0,1:T(8,128)(2,1)} async-done(((bf16[1024,4,1024]{2,0,1:T(8,128)(2,1)}), bf16[32,4,1024]{2,0,1:T(8,128)(2,1)}) %reduce-scatter.5.cloned.1.call-update) | async-done | bytes 262160 | tf_op jit(solution)/shard_map/reduce_scatter | solution.py:193
  (163 shorter events, 64.9 us)
Async XLA Ops:
  7.2 9.5 %copy-start = (bf16[1,1024,1024]{2,1,0:T(8,128)(2,1)S(1)}, bf16[1,1024,1024]{2,1,0:T(8,128)(2,1)}, u32[]{:S(2)}) copy-start(bf16[1,1024,1024]{2,1,0:T(8,128)(2,1)} %param.20) | copy-start | bytes 6291460
  7.2 478.8 %reduce-scatter.3.cloned.1.call-start = ((), (), s32[]{:S(2)}) async-start(), calls=%async_computation.2 | async-start | bytes 8650752 | tf_op jit(solution)/shard_map/reduce_scatter | solution.py:193
  16.7 3.2 copy-start.29
  16.7 14.2 %copy-start.37 = (s32[64]{0:T(128)S(1)}, s32[64]{0:T(128)}, u32[]{:S(2)}) copy-start(s32[64]{0:T(128)} %param.26) | copy-start | bytes 772
  16.7 14.5 %copy-start.36 = (s32[2,2]{1,0:T(2,128)S(1)}, s32[2,2]{1,0:T(2,128)}, u32[]{:S(2)}) copy-start(s32[2,2]{1,0:T(2,128)} %param.25) | copy-start | bytes 52
  18.7 1.2 copy-start.30
  19.9 34.6 %collective-permute-start = (bf16[2,128,1024]{2,1,0:T(8,128)(2,1)}, bf16[2,128,1024]{2,1,0:T(8,128)(2,1)}, u32[]{:S(2)}, u32[]{:S(2)}) collective-permute-start(bf16[2,128,1024]{2,1,0:T(8,128)(2,1)} %get-tuple-element.90), channel_id=1, source_target_pairs={{0,1},{1,2},{2,3},{3,4},{4,5},{5,6},{6,7},{7,8},{8,9},{9,10},{10,1... | collective-permute-start | bytes 1572872 | tf_op jit(solution)/shard_map/ppermute | solution.py:19
  21.5 33.0 %collective-permute-start.1 = (bf16[2,128,1024]{2,1,0:T(8,128)(2,1)}, bf16[2,128,1024]{2,1,0:T(8,128)(2,1)}, u32[]{:S(2)}, u32[]{:S(2)}) collective-permute-start(bf16[2,128,1024]{2,1,0:T(8,128)(2,1)} %get-tuple-element.91), channel_id=1, source_target_pairs={{0,31},{1,0},{2,1},{3,2},{4,3},{5,4},{6,5},{7,6},{8,7},{9,8},{10,9... | collective-permute-start | bytes 1572872 | tf_op jit(solution)/shard_map/ppermute | solution.py:19
  31.5 3.8 copy-start.23
  69.0 3.8 copy-start.35
  76.9 4.2 copy-start.39
  126.6 8.5 %copy-start.27 = (f32[1,128,1024]{2,1,0:T(8,128)S(1)}, f32[1,128,1024]{2,1,0:T(8,128)}, u32[]{:S(2)}) copy-start(f32[1,128,1024]{2,1,0:T(8,128)} %get-tuple-element.64) | copy-start | bytes 1572868
  126.6 8.4 %copy-start.28 = (f32[1,128,1024]{2,1,0:T(8,128)S(1)}, f32[1,128,1024]{2,1,0:T(8,128)}, u32[]{:S(2)}) copy-start(f32[1,128,1024]{2,1,0:T(8,128)} %get-tuple-element.65) | copy-start | bytes 1572868
  128.6 38.0 %collective-permute-start.2 = (bf16[2,128,1024]{2,1,0:T(8,128)(2,1)}, bf16[2,128,1024]{2,1,0:T(8,128)(2,1)}, u32[]{:S(2)}, u32[]{:S(2)}) collective-permute-start(bf16[2,128,1024]{2,1,0:T(8,128)(2,1)} %pad_maximum_fusion.10), channel_id=1, source_target_pairs={{0,31},{1,0},{2,1},{3,2},{4,3},{5,4},{6,5},{7,6},{8,7},{9,8},{10,9... | collective-permute-start | bytes 1572872 | tf_op jit(solution)/shard_map/ppermute | solution.py:19
  134.8 33.1 %collective-permute-start.3 = (bf16[2,128,1024]{2,1,0:T(8,128)(2,1)}, bf16[2,128,1024]{2,1,0:T(8,128)(2,1)}, u32[]{:S(2)}, u32[]{:S(2)}) collective-permute-start(bf16[2,128,1024]{2,1,0:T(8,128)(2,1)} %pad_maximum_fusion.11), channel_id=1, source_target_pairs={{0,1},{1,2},{2,3},{3,4},{4,5},{5,6},{6,7},{7,8},{8,9},{9,10},{10,1... | collective-permute-start | bytes 1572872 | tf_op jit(solution)/shard_map/ppermute | solution.py:19
  162.1 4.6 copy-start.7
  162.1 4.6 copy-start.9
  169.4 0.8 copy-start.18
  174.0 6.4 copy-start.11
  187.2 566.7 %reduce-scatter.5.cloned.1.call-start = ((), (), s32[]{:S(2)}) async-start(), calls=%async_computation.3 | async-start | bytes 8650752 | tf_op jit(solution)/shard_map/reduce_scatter | solution.py:193
  189.8 3.1 copy-start.31
  191.8 1.1 copy-start.32
  193.0 21.5 %collective-permute-start.4 = (bf16[2,128,1024]{2,1,0:T(8,128)(2,1)}, bf16[2,128,1024]{2,1,0:T(8,128)(2,1)}, u32[]{:S(2)}, u32[]{:S(2)}) collective-permute-start(bf16[2,128,1024]{2,1,0:T(8,128)(2,1)} %get-tuple-element.88), channel_id=1, source_target_pairs={{0,1},{1,2},{2,3},{3,4},{4,5},{5,6},{6,7},{7,8},{8,9},{9,10},{10,1... | collective-permute-start | bytes 1572872 | tf_op jit(solution)/shard_map/ppermute | solution.py:19
  193.0 41.6 %collective-permute-start.5 = (bf16[2,128,1024]{2,1,0:T(8,128)(2,1)}, bf16[2,128,1024]{2,1,0:T(8,128)(2,1)}, u32[]{:S(2)}, u32[]{:S(2)}) collective-permute-start(bf16[2,128,1024]{2,1,0:T(8,128)(2,1)} %get-tuple-element.89), channel_id=1, source_target_pairs={{0,31},{1,0},{2,1},{3,2},{4,3},{5,4},{6,5},{7,6},{8,7},{9,8},{10,9... | collective-permute-start | bytes 1572872 | tf_op jit(solution)/shard_map/ppermute | solution.py:19
  246.1 2.9 copy-start.14
  252.4 4.4 copy-start.19
  256.8 2.5 copy-start.3
  256.8 2.5 copy-start.22
  259.3 1.0 copy-start.24
  259.3 3.6 copy-start.38
  260.3 2.7 copy-start.13
  260.7 4.0 copy-start.25
  260.7 18.4 %collective-permute-start.6 = (bf16[256,1024]{1,0:T(8,128)(2,1)S(1)}, bf16[256,1024]{1,0:T(8,128)(2,1)}, u32[]{:S(2)}, u32[]{:S(2)}) collective-permute-start(bf16[256,1024]{1,0:T(8,128)(2,1)S(1)} %fusion.159), channel_id=1, source_target_pairs={{32,0},{64,32},{96,64},{128,96},{160,128},{192,160},{224,192},{33,... | collective-permute-start | bytes 1572872 | tf_op jit(solution)/shard_map/ppermute | solution.py:25
  263.0 16.1 %copy-start.33 = (bf16[1,256,1024]{2,1,0:T(8,128)(2,1)S(1)}, bf16[1,256,1024]{2,1,0:T(8,128)(2,1)}, u32[]{:S(2)}) copy-start(bf16[1,256,1024]{2,1,0:T(8,128)(2,1)} %param.24) | copy-start | bytes 1572868
  280.2 2.7 copy-start.16
  295.7 3.7 copy-start.34
  325.3 2.9 copy-start.1
  328.5 14.9 %copy-start.2 = (f32[2,3,128,1024]{3,2,1,0:T(8,128)S(1)}, f32[2,3,128,1024]{3,2,1,0:T(8,128)}, u32[]{:S(2)}) copy-start(f32[2,3,128,1024]{3,2,1,0:T(8,128)} %reshape.353) | copy-start | bytes 9437188
  329.4 49.6 %collective-permute-start.7 = (bf16[2,128,1024]{2,1,0:T(8,128)(2,1)}, bf16[2,128,1024]{2,1,0:T(8,128)(2,1)}, u32[]{:S(2)}, u32[]{:S(2)}) collective-permute-start(bf16[2,128,1024]{2,1,0:T(8,128)(2,1)} %pad_maximum_fusion.12), channel_id=1, source_target_pairs={{0,31},{1,0},{2,1},{3,2},{4,3},{5,4},{6,5},{7,6},{8,7},{9,8},{10,9... | collective-permute-start | bytes 1572872 | tf_op jit(solution)/shard_map/ppermute | solution.py:19
  343.2 42.9 %collective-permute-start.8 = (bf16[2,128,1024]{2,1,0:T(8,128)(2,1)}, bf16[2,128,1024]{2,1,0:T(8,128)(2,1)}, u32[]{:S(2)}, u32[]{:S(2)}) collective-permute-start(bf16[2,128,1024]{2,1,0:T(8,128)(2,1)} %pad_maximum_fusion.13), channel_id=1, source_target_pairs={{0,1},{1,2},{2,3},{3,4},{4,5},{5,6},{6,7},{7,8},{8,9},{9,10},{10,1... | collective-permute-start | bytes 1572872 | tf_op jit(solution)/shard_map/ppermute | solution.py:19
  363.6 1.0 copy-start.5
  368.2 10.8 %copy-start.6 = (f32[1,2,128,1024]{3,2,0,1:T(8,128)S(1)}, f32[1,2,128,1024]{3,2,0,1:T(8,128)}, u32[]{:S(2)}) copy-start(f32[1,2,128,1024]{3,2,0,1:T(8,128)} %copy-done.5) | copy-start | bytes 3145732
  368.2 10.8 %copy-start.10 = (f32[2,2,128,1024]{3,2,0,1:T(8,128)S(1)}, f32[2,2,128,1024]{3,2,0,1:T(8,128)}, u32[]{:S(2)}) copy-start(f32[2,2,128,1024]{3,2,0,1:T(8,128)} %pad_maximum_fusion.5) | copy-start | bytes 6291460
  387.6 0.8 copy-start.20
  392.3 6.4 copy-start.12
  405.4 1.0 copy-start.15
  406.4 2.5 copy-start.8
  406.4 2.5 copy-start.21
  408.9 1.4 copy-start.4
  410.4 1.0 copy-start.17
  411.3 1.1 copy-start.26
Sparse Core Ops, SparseCore 0:
  187.3 298.5 reduce-scatter.2
  488.5 265.3 reduce-scatter.4
where the time goes:
time: 767 us; the launch traced here: 763 us
  waiting for transfers between devices  408 us (53%)
  matrix products  148 us (19%)
  local copies, waits for them, and re-layouts  90.6 us (12%)
  other arithmetic  54.7 us (7%)
  starting transfers between devices  42.5 us (6%)
  between operations  18.9 us (2%)
    reduce_scatter x2, waiting for transfers between devices, per_device(): lax.psum_scatter(tick_rows(jnp.int32(0), features // part_count * lax.axi...  341 us
    ppermute x8, waiting for transfers between devices, from_behind(): return lax.ppermute(value, axis, pairs)  55.5 us
    ppermute x8, starting transfers between devices, from_behind(): return lax.ppermute(value, axis, pairs)  40.2 us
    dot_general x2, matrix products, per_device(): jnp.einsum('bhqk,bqhd->bkhd', scores_bf, query_heads, preferred_element_t...  35.7 us
    dot_general x2, matrix products, per_device(): jnp.einsum('bhqk,bkhd->bqhd', scores_bf, key_heads, preferred_element_typ...  34.5 us
    dot_general x4, matrix products, left_dot(): lax.dot_general(left, right, (((0,), (0,)), ((), ())), preferred_element_...  19.4 us
    unnamed x92, local copies, waits for them, and re-layouts  19.1 us
    dot_general x8, matrix products, right_dot(): lax.dot_general(left, right, (((1,), (1,)), ((), ())), preferred_element_...  15.8 us
  transfers between devices with their start and end apart: 11, of which 8 were waited for; matrix products, arithmetic and copies ran while one was open for 24% of the time, Pallas kernels for 0%

commit v1 on v0

v1 whole, which is shorter than its diff:
```python
import functools
import math

import jax
import jax.numpy as jnp
from jax import lax
from jax.experimental import pallas as pl
from jax.experimental.pallas import tpu as pltpu
from jax.sharding import PartitionSpec as P

HEADS = 8
BLOCK = 128
ROWS = 256
WIDE = 1024
HEAD_DIM = 128
TILE = 256
STEPS = WIDE // TILE
EPSILON = 1e-06
SCALE = 1.0 / math.sqrt(HEAD_DIM)
PARTS = 32
UNLISTED = 3e38
BF = jnp.bfloat16
F32 = jnp.float32

AX, BX, AY, BY, ZZ = 8, 24, 1, 3, 4
ORDERS = (
    (AX, AY, BX, BY, ZZ),
    (BX, BY, AX, AY, ZZ),
    (AY, AX, BY, BX, ZZ),
    (BY, BX, AY, AX, ZZ),
)


def right_dot(left, right):
    return lax.dot_general(
        left, right, (((1,), (1,)), ((), ())), preferred_element_type=jnp.float32
    )


def left_dot(left, right):
    return lax.dot_general(
        left, right, (((0,), (0,)), ((), ())), preferred_element_type=jnp.float32
    )


def dot(left, right):
    return jnp.dot(left, right, preferred_element_type=jnp.float32)


def inverse_rms(x):
    return lax.rsqrt(jnp.mean(x * x, axis=-1, keepdims=True) + EPSILON)


def params():
    return pltpu.CompilerParams(
        dimension_semantics=("arbitrary",), vmem_limit_bytes=40 * 1024 * 1024
    )


def cost(flops, moved):
    return pl.CostEstimate(flops=int(flops), bytes_accessed=int(moved), transcendentals=0)


def shape(rows, columns, dtype=BF):
    return jax.ShapeDtypeStruct((rows, columns), dtype)


def whole(rows, columns=WIDE):
    return pl.BlockSpec((rows, columns), lambda i, info: (0, 0))


def part_of(rows, at=0):
    return pl.BlockSpec((rows, TILE), lambda i, info: (at, i))


def member_block(tick):
    return pl.BlockSpec((1, ROWS, WIDE), lambda i, info: (info[tick], 0, 0))


WEIGHT = pl.BlockSpec((WIDE, TILE), lambda i, info: (0, i))
WEIGHT_ROWS = pl.BlockSpec((TILE, WIDE), lambda i, info: (i, 0))


def call(kernel, info, args, in_specs, out_shape, out_specs, scratch, estimate, name):
    return pl.pallas_call(
        kernel,
        out_shape=out_shape,
        grid_spec=pltpu.PrefetchScalarGridSpec(
            num_scalar_prefetch=1,
            grid=(STEPS,),
            in_specs=in_specs,
            out_specs=out_specs,
            scratch_shapes=scratch,
        ),
        compiler_params=params(),
        cost_estimate=estimate,
        name=name,
    )(info, *args)


def project_kernel(info, xa, xb, wq, wk, wv, normed, q, k, v):
    rows = normed.shape[0] // 2

    @pl.when(pl.program_id(0) == 0)
    def _():
        for at, ref in enumerate((xa, xb)):
            x = (ref[0] if len(ref.shape) == 3 else ref[...]).astype(F32)
            normed[at * rows : (at + 1) * rows, :] = (x * inverse_rms(x)).astype(BF)

    n = normed[...]
    q[...] = dot(n, wq[...]).astype(BF)
    k[...] = dot(n, wk[...]).astype(BF)
    v[...] = dot(n, wv[...]).astype(BF)


def project(info, xs, x_specs, weights, name):
    rows = 2 * xs[0].shape[-2]
    return call(
        project_kernel,
        info,
        (*xs, *weights),
        [*x_specs, WEIGHT, WEIGHT, WEIGHT],
        [shape(rows, WIDE)] * 4,
        [whole(rows), part_of(rows), part_of(rows), part_of(rows)],
        [],
        cost(6 * rows * WIDE * WIDE, 6 * WIDE * WIDE + 10 * rows * WIDE),
        name,
    )


def attend_kernel(info, q, k, v, kh, vh, g, wo, att, dq, dk, dv, stats):
    step = pl.program_id(0)
    ga = right_dot(g[...], wo[...]).astype(BF)
    column = lax.broadcasted_iota(jnp.int32, (1, 3 * BLOCK), 1)
    lane = lax.broadcasted_iota(jnp.int32, (BLOCK, HEAD_DIM), 1)

    @pl.when(step == 0)
    def _():
        stats[...] = jnp.zeros_like(stats)

    valid = []
    listed = []
    for b in range(2):
        limit = [info[2 + 3 * b + e] for e in range(3)]
        inside = (column < limit[0]) & (column < BLOCK)
        for e in (1, 2):
            at = column - e * BLOCK
            inside = inside | ((at >= 0) & (at < limit[e]) & (at < BLOCK))
        valid.append(inside)
        listed.append(limit[2 * b] > 0)
    for hh in range(2):
        sl = slice(hh * HEAD_DIM, (hh + 1) * HEAD_DIM)
        head = step * 2 + hh
        kx = jnp.concatenate([kh[:BLOCK, sl], k[:, sl], kh[BLOCK:, sl]], axis=0)
        vx = jnp.concatenate([vh[:BLOCK, sl], v[:, sl], vh[BLOCK:, sl]], axis=0)
        dk_sum = None
        for b in range(2):
            rows = slice(b * BLOCK, (b + 1) * BLOCK)
            qb, gb = q[rows, sl], ga[rows, sl]
            kb, vb = kx[b * BLOCK : (b + 3) * BLOCK], vx[b * BLOCK : (b + 3) * BLOCK]
            s = jnp.where(valid[b], right_dot(qb, kb) * SCALE, -jnp.inf)
            peak = jnp.max(s, axis=-1, keepdims=True)
            raised = jnp.exp(s - peak)
            total = jnp.sum(raised, axis=-1, keepdims=True)
            p = raised * (1.0 / total)
            pb = p.astype(BF)
            att[rows, sl] = dot(pb, vb).astype(BF)
            gp = right_dot(gb, vb)
            mid = jnp.sum(p * gp, axis=-1, keepdims=True)
            ds = (p * (gp - mid) * SCALE).astype(BF)
            dq[rows, sl] = dot(ds, kb).astype(BF)
            own = slice(BLOCK, 3 * BLOCK) if b == 0 else slice(0, 2 * BLOCK)
            dk_now = left_dot(ds[:, own], qb)
            dv_now = left_dot(pb[:, own], gb)
            dk_sum, dv_sum = (
                (dk_now, dv_now) if dk_sum is None else (dk_sum + dk_now, dv_sum + dv_now)
            )
            sent_peak = jnp.where(listed[b], peak, UNLISTED)
            now = stats[rows, :]
            now = jnp.where(lane == head, sent_peak, now)
            now = jnp.where(lane == HEADS + head, total, now)
            stats[rows, :] = jnp.where(lane == 2 * HEADS + head, mid, now)
        dk[:, sl] = dk_sum
        dv[:, sl] = dv_sum


def attend(info, tick, q, k, v, kh, vh, g, wo):
    own = part_of(ROWS, tick)
    return call(
        attend_kernel,
        info,
        (q, k, v, kh, vh, g, wo),
        [own, own, own, part_of(ROWS), part_of(ROWS), whole(ROWS), WEIGHT_ROWS],
        [shape(ROWS, WIDE)] * 2 + [shape(ROWS, WIDE, F32)] * 2 + [shape(ROWS, HEAD_DIM, F32)],
        [part_of(ROWS)] * 4 + [whole(ROWS, HEAD_DIM)],
        [],
        cost(6 * 2 * ROWS * WIDE * WIDE, 12 * ROWS * WIDE * 2),
        f"attend{tick}",
    )


def finish_kernel(
    info, qh, g_prev, g_next, wo, k, v, s_prev, s_next, dq, dk, dv, wq, wk, wv, x, g, gk, gv, gx, gn
):
    step = pl.program_id(0)
    gah = right_dot(jnp.concatenate([g_prev[...], g_next[...]], axis=0), wo[...]).astype(BF)
    lane = lax.broadcasted_iota(jnp.int32, (BLOCK, HEAD_DIM), 1)
    column = lax.broadcasted_iota(jnp.int32, (1, BLOCK), 1)
    for hh in range(2):
        sl = slice(hh * HEAD_DIM, (hh + 1) * HEAD_DIM)
        head = step * 2 + hh
        for b, stats in enumerate((s_prev, s_next)):
            rows = slice(b * BLOCK, (b + 1) * BLOCK)

            def pick(at, stats=stats, head=head):
                chosen = jnp.where(lane == at * HEADS + head, stats[...], 0.0)
                return jnp.sum(chosen, axis=-1, keepdims=True)

            qb, kb, vb, gb = qh[rows, sl], k[rows, sl], v[rows, sl], gah[rows, sl]
            s = right_dot(qb, kb) * SCALE
            inside = column < info[3 + 3 * b]
            p = jnp.where(inside, jnp.exp(s - pick(0)), 0.0) * (1.0 / pick(1))
            ds = (p * (right_dot(gb, vb) - pick(2)) * SCALE).astype(BF)
            dk_far = left_dot(ds, qb).astype(BF).astype(F32)
            dv_far = left_dot(p.astype(BF), gb).astype(BF).astype(F32)
            gk[rows, sl] = (dk[rows, sl] + dk_far).astype(BF)
            gv[rows, sl] = (dv[rows, sl] + dv_far).astype(BF)
    now = (
        right_dot(dq[...], wq[...]) + right_dot(gk[...], wk[...]) + right_dot(gv[...], wv[...])
    )

    @pl.when(step == 0)
    def _():
        gn[...] = now

    @pl.when(step > 0)
    def _():
        gn[...] += now

    @pl.when(step == STEPS - 1)
    def _():
        xf = x[0].astype(F32)
        r = inverse_rms(xf)
        xr = xf * r
        grad = gn[...]
        grad_in = r * (grad - xr * jnp.mean(grad * xr, axis=-1, keepdims=True))
        gx[...] = (g[...].astype(F32) + grad_in).astype(BF)


def finish(info, tick, qh, g_edges, wo, k, v, stats, dq, dk, dv, weights, x, g):
    own, here = part_of(ROWS, tick), part_of(ROWS)
    edge, side = whole(BLOCK), whole(BLOCK, HEAD_DIM)
    return call(
        finish_kernel,
        info,
        (qh, *g_edges, wo, k, v, *stats, dq, dk, dv, *weights, x, g),
        [here, edge, edge, WEIGHT_ROWS, own, own, side, side, here, here, here]
        + [WEIGHT, WEIGHT, WEIGHT, member_block(tick), whole(ROWS)],
        [shape(ROWS, WIDE)] * 3,
        [here, here, whole(ROWS)],
        [pltpu.VMEM((ROWS, WIDE), F32)],
        cost(10 * ROWS * WIDE * WIDE, 8 * WIDE * WIDE + 20 * ROWS * WIDE),
        f"finish{tick}",
    )


def position(order, q):
    found = 0
    for bit, mask in enumerate(order):
        if (q >> (len(order) - 1 - bit)) & 1:
            found ^= mask
    return found


def weight_kernel(order, info, la, lb, ra, rb, keep, send, chunks):
    product = left_dot(la[...], ra[...]) + left_dot(lb[...], rb[...])
    chunks[...] = product.astype(BF).reshape(chunks.shape)
    me = info[8]
    half = PARTS // 2
    for q in range(PARTS):
        out = keep if q < half else send
        out[q % half] = chunks[lax.bitwise_xor(jnp.int32(position(order, q)), me)]


def weight_part(info, order, left, left_at, right, name):
    depth = WIDE // PARTS
    half = jax.ShapeDtypeStruct((PARTS // 2, depth, WIDE), BF)
    half_spec = pl.BlockSpec((PARTS // 2, depth, TILE), lambda i, info: (0, 0, i))

    def rows_at(at):
        return pl.BlockSpec((ROWS, WIDE), lambda i, info: (at, 0))

    return call(
        functools.partial(weight_kernel, order),
        info,
        (*left, *right),
        [rows_at(left_at[0]), rows_at(left_at[1]), part_of(ROWS), part_of(ROWS)],
        [half, half],
        [half_spec, half_spec],
        [pltpu.VMEM((PARTS, depth, TILE), BF)],
        cost(4 * ROWS * WIDE * WIDE, 8 * ROWS * WIDE + 2 * WIDE * WIDE),
        name,
    )


def swap(value, mask):
    return lax.ppermute(value, "mesh", [(p, p ^ mask) for p in range(PARTS)])


def add(left, right):
    return (left.astype(F32) + right.astype(F32)).astype(BF)


def ring(value, steps):
    return lax.ppermute(value, "mesh", [(p, (p + steps) % PARTS) for p in range(PARTS)])


def from_above(value, sections, steps):
    pairs = [
        (s * PARTS + p, (s - 1) * PARTS + (p + steps) % PARTS)
        for s in range(1, sections)
        for p in range(PARTS)
    ]
    return lax.ppermute(value, ("section", "mesh"), pairs)


def top_ring(value, sections, steps):
    base = (sections - 1) * PARTS
    pairs = [(base + p, base + (p + steps) % PARTS) for p in range(PARTS)]
    return lax.ppermute(value, ("section", "mesh"), pairs)


def per_device(
    saved_inputs, w_query, w_key, w_value, w_out, pending, top_grads, key_blocks, counts, plan
):
    sections = lax.axis_size("section")
    section_here = lax.axis_index("section")
    part_here = lax.axis_index("mesh")
    weights = (w_query[0], w_key[0], w_value[0])
    wo = w_out[0]
    saved = saved_inputs[0]
    members = lax.dynamic_slice_in_dim(plan, section_here, 1, axis=1)[:, 0]
    own_counts = lax.dynamic_slice_in_dim(counts, part_here * 2, 2)
    listed = jnp.where(key_blocks >= 0, counts[jnp.maximum(key_blocks, 0)], 0)
    limits = jnp.stack([listed[:, 1], own_counts, listed[:, 0]], axis=1)
    info = jnp.concatenate(
        [members, limits.reshape(6), part_here[None].astype(jnp.int32)]
    ).astype(jnp.int32)

    def edge(tick, at):
        return lax.dynamic_slice(
            saved, (members[tick], jnp.int32(at), jnp.int32(0)), (1, BLOCK, WIDE)
        )[0]

    g0 = pending[0]
    top = top_grads[0]
    last, first = ROWS - BLOCK, 0
    x_edges0 = (ring(edge(0, last), 1), ring(edge(0, first), -1))
    later = (edge(1, last), edge(1, first), g0[last:], g0[:BLOCK], top[last:], top[:BLOCK])
    x_edges0, later = lax.optimization_barrier((x_edges0, later))
    g_edges0 = (ring(later[2], 1), ring(later[3], -1))
    x_edges1 = (ring(later[0], 1), ring(later[1], -1))
    top_edges = (top_ring(later[4], sections, 1), top_ring(later[5], sections, -1))

    normed, q, k, v = project(
        info, (saved, saved), (member_block(0), member_block(1)), weights, "project_own"
    )
    is_top = section_here == sections - 1
    g, g_edges = g0, g_edges0
    outgoing, attended, grads = [], [], []
    for tick in range(2):
        x_edges = (x_edges0, x_edges1)[tick]
        _, qh, kh, vh = project(
            info, x_edges, (whole(BLOCK), whole(BLOCK)), weights, f"project_edge{tick}"
        )
        if tick == 1:
            grad_x = outgoing[0]
            passed = from_above(grad_x, sections, 0)
            passed_prev = from_above(grad_x[last:], sections, 1)
            passed_next = from_above(grad_x[:BLOCK], sections, -1)
            g = jnp.where(is_top, top, passed)
            g_edges = (
                jnp.where(is_top, top_edges[0], passed_prev),
                jnp.where(is_top, top_edges[1], passed_next),
            )
        att, dq, dk, dv, stats = attend(info, tick, q, k, v, kh, vh, g, wo)
        far = (ring(stats[BLOCK:], 1), ring(stats[:BLOCK], -1))
        gk, gv, gx = finish(
            info, tick, qh, g_edges, wo, k, v, far, dq, dk, dv, weights, saved, g
        )
        outgoing.append(gx)
        attended.append(att)
        grads.append((dq, gk, gv, g))

    sums = []
    for w in (3, 0, 1, 2):
        left = attended if w == 3 else (normed, normed)
        left_at = (0, 0) if w == 3 else (0, 1)
        right = (grads[0][w], grads[1][w])
        keep, send = weight_part(info, ORDERS[w], left, left_at, right, f"weight{w}")
        sums.append((w, keep, send))
    for stage in range(4):
        following = []
        for w, keep, send in sums:
            received = swap(send, ORDERS[w][stage])
            half = keep.shape[0] // 2
            following.append(
                (w, add(keep[:half], received[:half]), add(keep[half:], received[half:]))
            )
        sums = following
    sums.sort(key=lambda item: item[0])
    kept = jnp.stack([item[1][0] for item in sums], axis=1)
    sent = jnp.stack([item[2][0] for item in sums], axis=1)
    layer_total = kept.astype(F32) + swap(sent, ZZ).astype(F32)
    return (layer_total[None], jnp.stack(outgoing)[:, None])


def solution(mesh):
    in_specs = (
        P("section", None, "mesh", None),
        P("section", None, None),
        P("section", None, None),
        P("section", None, None),
        P("section", None, None),
        P("section", "mesh", None),
        P(None, "mesh", None),
        P("mesh", None),
        P(),
        P(),
    )
    out_specs = (P("section", "mesh", None, None), P(None, "section", "mesh", None))
    return jax.shard_map(
        per_device, mesh=mesh, in_specs=in_specs, out_specs=out_specs, check_vma=False
    )
```

time: 767 us -> 248 us (0.32)
  waiting for transfers between devices: 408 us -> 83.4 us
  matrix products: 148 us -> 0 us
  Pallas kernels: 0 us -> 81.5 us
  local copies, waits for them, and re-layouts: 90.6 us -> 16.5 us
  other arithmetic: 54.7 us -> 5.42 us
  between operations: 18.9 us -> 5.25 us
  starting transfers between devices: 42.5 us -> 55.8 us
    reduce_scatter x2 -> x0, waiting for transfers between devices: 341 us -> none  [per_device(): lax.psum_scatter(tick_rows(jnp.int32(0), features // part_count * lax.axi...]
    dot_general x28 -> x0, matrix products: 140 us -> none  [the longest x2 35.7 us: per_device(): jnp.einsum('bhqk,bqhd->bkhd', scores_bf, query_heads, preferred_element_t...]
    pallas_call x0 -> x11, Pallas kernels: none -> 81.5 us  [call(): pl.pallas_call(kernel, out_shape=out_shape, grid_spec=pltpu.PrefetchScala...]
    another operation x18 -> x6, other arithmetic: 23.6 us -> 0.25 us  [the longest x4 0.14 us: per_device(): kept = jnp.stack([item[1][0] for item in sums], axis=1)]
    reshape x8 -> x1, local copies, waits for them, and re-layouts: 21.3 us -> 0.08 us  [per_device(): limits.reshape(6)]
    concatenate x4 -> x1, other arithmetic: 16.9 us -> 0.08 us  [per_device(): jnp.concatenate([members, limits.reshape(6), part_here[None].astype(jnp.i...]
    ppermute x9 -> x32, waiting for transfers between devices: 67.8 us -> 83.4 us  [the longest x17 53.9 us: swap(): return lax.ppermute(value, 'mesh', [(p, p ^ mask) for p in range(PARTS)])]
    transpose x4 -> x0, local copies, waits for them, and re-layouts: 14.3 us -> none  [the longest x2 7.14 us: per_device(): jnp.einsum('bhqk,bqhd->bkhd', probs_bf, grad_heads, preferred_element_typ...]
  transfers between devices with their start and end apart: 11 -> 32, of which waited for: 8 -> 15; matrix products, arithmetic and copies ran while one was open for 24% -> 3% of each run, Pallas kernels for 0% -> 26%
where the time goes in v1:
time: 248 us
  waiting for transfers between devices  83.4 us (34%)
  Pallas kernels  81.5 us (33%)
  starting transfers between devices  55.8 us (22%)
  local copies, waits for them, and re-layouts  16.5 us (7%)
  other arithmetic  5.42 us (2%)
  between operations  5.25 us (2%)
    pallas_call x11, Pallas kernels, call(): pl.pallas_call(kernel, out_shape=out_shape, grid_spec=pltpu.PrefetchScala...  81.5 us
    ppermute x17, waiting for transfers between devices, swap(): return lax.ppermute(value, 'mesh', [(p, p ^ mask) for p in range(PARTS)])  53.9 us
    ppermute x10, starting transfers between devices, ring(): lax.ppermute(value, 'mesh', [(p, (p + steps) % PARTS) for p in range(PART...  33.6 us
    ppermute x10, waiting for transfers between devices, ring(): lax.ppermute(value, 'mesh', [(p, (p + steps) % PARTS) for p in range(PART...  20.8 us
    ppermute x17, starting transfers between devices, swap(): return lax.ppermute(value, 'mesh', [(p, p ^ mask) for p in range(PARTS)])  12.2 us
    unnamed x65, local copies, waits for them, and re-layouts  9.81 us
    ppermute x3, waiting for transfers between devices, from_above(): return lax.ppermute(value, ('section', 'mesh'), pairs)  8.74 us
    ppermute x3, starting transfers between devices, from_above(): return lax.ppermute(value, ('section', 'mesh'), pairs)  7.93 us
  transfers between devices with their start and end apart: 32, of which 15 were waited for; matrix products, arithmetic and copies ran while one was open for 3% of the time, Pallas kernels for 26%

profile of v1, /device:TPU:32, one launch (start us, length us, event | category | flops | bytes accessed | tf_op | source)
XLA Modules:
  0.0 247.9 jit_solution(13361555910734910666)
XLA Ops:
  0.7 1.0 fusion.8
  1.7 0.5 fusion.12
  6.1 2.2 dynamic-slice_bitcast_fusion
  8.3 10.9 %collective-permute-start.1 = (bf16[128,1024]{1,0:T(8,128)(2,1)}, bf16[128,1024]{1,0:T(8,128)(2,1)S(1)}, u32[]{:S(2)}, u32[]{:S(2)}) collective-permute-start(bf16[128,1024]{1,0:T(8,128)(2,1)} %get-tuple-element.101), channel_id=1, source_target_pairs={{0,31},{1,0},{2,1},{3,2},{4,3},{5,4},{6,5},{7,6},{8,7},{9,8},{10,9... | collective-permute-start | bytes 786440 | tf_op jit(solution)/shard_map/ppermute | solution.py:315
  19.5 0.6 gather_fusion
  20.5 1.6 copy-done.2
  22.1 1.6 copy-done.4
  23.7 1.4 copy-done.6
  25.1 6.0 %project_own.1 = (bf16[512,1024]{1,0:T(8,128)(2,1)S(1)}, bf16[512,1024]{1,0:T(8,128)(2,1)S(1)}, bf16[512,1024]{1,0:T(8,128)(2,1)S(1)}, bf16[512,1024]{1,0:T(8,128)(2,1)S(1)}) custom-call(s32[9]{0:T(128)S(1)} %pad_add_fusion.1.info, bf16[3,256,1024]{2,1,0:T(8,128)(2,1)S(1)} %bitcast.68, bf16[3,256,1024]{2,1,0:T(8,128)(2,1)S(1)} %bitcast.69, ...), custom_call_target="tpu_custom_call" | custom-call | flops 3221225472 | bytes 11534336 | tf_op jit(solution)/shard_map/project_own/pallas_call | solution.py:85
  31.2 1.0 slice_bitcast_fusion
  32.2 8.9 %collective-permute-done.xa = bf16[128,1024]{1,0:T(8,128)(2,1)} collective-permute-done((bf16[128,1024]{1,0:T(8,128)(2,1)}, bf16[128,1024]{1,0:T(8,128)(2,1)}, u32[]{:S(2)}, u32[]{:S(2)}) %collective-permute-start) | collective-permute-done | bytes 262176 | tf_op jit(solution)/shard_map/ppermute | solution.py:315
  41.2 10.1 %collective-permute-start.5 = (bf16[128,1024]{1,0:T(8,128)(2,1)S(1)}, bf16[128,1024]{1,0:T(8,128)(2,1)S(1)}, u32[]{:S(2)}, u32[]{:S(2)}) collective-permute-start(bf16[128,1024]{1,0:T(8,128)(2,1)S(1)} %get-tuple-element.59), channel_id=1, source_target_pairs={{0,31},{1,0},{2,1},{3,2},{4,3},{5,4},{6,5},{7,6},{8,7},{9,8},{10,9... | collective-permute-start | bytes 786440 | tf_op jit(solution)/shard_map/ppermute | solution.py:315
  51.3 5.3 %project_edge0.1 = (bf16[256,1024]{1,0:T(8,128)(2,1)}, bf16[256,1024]{1,0:T(8,128)(2,1)S(1)}, bf16[256,1024]{1,0:T(8,128)(2,1)S(1)}, bf16[256,1024]{1,0:T(8,128)(2,1)S(1)}) custom-call(s32[9]{0:T(128)S(1)} %pad_add_fusion.1.info, bf16[128,1024]{1,0:T(8,128)(2,1)} %collective-permute-done.xa, bf16[128,1024]{1,0:T(8,128)(2,1)S(1)} %collective-permute-done.1.xb, ...), custom_call_target="tpu_custom_call" | custom-call | flops 1610612736 | bytes 8912896 | tf_op jit(solution)/shard_map/project_edge0/pallas_call | solution.py:85
  56.6 14.5 %attend0.1 = (bf16[256,1024]{1,0:T(8,128)(2,1)S(1)}, bf16[256,1024]{1,0:T(8,128)(2,1)S(1)}, f32[256,1024]{1,0:T(8,128)S(1)}, f32[256,1024]{1,0:T(8,128)S(1)}, f32[256,128]{1,0:T(8,128)S(1)}) custom-call(s32[9]{0:T(128)S(1)} %pad_add_fusion.1.info, bf16[512,1024]{1,0:T(8,128)(2,1)S(1)} %get-tuple-element.45.q, bf16[512,1024]{1,0:T(8,128)(2,1)S(1)} %get-tuple-element.46.k, ...), custom_call_target="tpu_custom_call" | custom-call | flops 3221225472 | bytes 6291456 | tf_op jit(solution)/shard_map/attend0/pallas_call | solution.py:85
  71.3 2.0 collective-permute-start.6
  73.3 2.2 collective-permute-done.7.s_next
  75.5 8.3 %collective-permute-start.3 = (bf16[128,1024]{1,0:T(8,128)(2,1)}, bf16[128,1024]{1,0:T(8,128)(2,1)}, u32[]{:S(2)}, u32[]{:S(2)}) collective-permute-start(bf16[128,1024]{1,0:T(8,128)(2,1)} %get-tuple-element.54), channel_id=1, source_target_pairs={{0,31},{1,0},{2,1},{3,2},{4,3},{5,4},{6,5},{7,6},{8,7},{9,8},{10,9... | collective-permute-start | bytes 786440 | tf_op jit(solution)/shard_map/ppermute | solution.py:315
  83.8 0.6 collective-permute-done.6.s_prev
  84.5 1.4 collective-permute-start.15
  85.9 11.3 %finish0.1 = (bf16[256,1024]{1,0:T(8,128)(2,1)S(1)}, bf16[256,1024]{1,0:T(8,128)(2,1)S(1)}, bf16[256,1024]{1,0:T(8,128)(2,1)S(1)}) custom-call(s32[9]{0:T(128)S(1)} %pad_add_fusion.1.info, bf16[256,1024]{1,0:T(8,128)(2,1)S(1)} %get-tuple-element.57.qh, bf16[128,1024]{1,0:T(8,128)(2,1)S(1)} %collective-permute-done.4.g_prev, ...), custom_call_target="tpu_custom_call" | custom-call | flops 2684354560 | bytes 13631488 | tf_op jit(solution)/shard_map/finish0/pallas_call | solution.py:85
  97.3 0.8 copy-done.15
  98.0 0.8 fusion.9
  98.9 1.9 collective-permute-start.16
  100.8 0.7 collective-permute-start.13
  101.5 2.5 %collective-permute-start.8 = (bf16[256,1024]{1,0:T(8,128)(2,1)}, bf16[256,1024]{1,0:T(8,128)(2,1)S(1)}, u32[]{:S(2)}, u32[]{:S(2)}) collective-permute-start(bf16[256,1024]{1,0:T(8,128)(2,1)} %copy-done.15), channel_id=1, source_target_pairs={{32,0},{33,1},{34,2},{35,3},{36,4},{37,5},{38,6},{39,7},{40,8},{41... | collective-permute-start | bytes 1572872 | tf_op jit(solution)/shard_map/ppermute | solution.py:324
  104.0 3.5 %collective-permute-start.14 = (bf16[128,1024]{1,0:T(8,128)(2,1)}, bf16[128,1024]{1,0:T(8,128)(2,1)S(1)}, u32[]{:S(2)}, u32[]{:S(2)}) collective-permute-start(bf16[128,1024]{1,0:T(8,128)(2,1)} %get-tuple-element.119), channel_id=1, source_target_pairs={{32,1},{33,2},{34,3},{35,4},{36,5},{37,6},{38,7},{39,8},{40,9},{41... | collective-permute-start | bytes 786440 | tf_op jit(solution)/shard_map/ppermute | solution.py:324
  107.6 1.6 copy-done.3
  109.2 1.6 copy-done.5
  110.7 5.4 %project_edge1.1 = (bf16[256,1024]{1,0:T(8,128)(2,1)}, bf16[256,1024]{1,0:T(8,128)(2,1)S(1)}, bf16[256,1024]{1,0:T(8,128)(2,1)S(1)}, bf16[256,1024]{1,0:T(8,128)(2,1)S(1)}) custom-call(s32[9]{0:T(128)S(1)} %pad_add_fusion.1.info, bf16[128,1024]{1,0:T(8,128)(2,1)S(1)} %collective-permute-done.2.xa, bf16[128,1024]{1,0:T(8,128)(2,1)} %collective-permute-done.3.xb, ...), custom_call_target="tpu_custom_call" | custom-call | flops 1610612736 | bytes 8912896 | tf_op jit(solution)/shard_map/project_edge1/pallas_call | solution.py:85
  116.1 1.1 broadcast_select_fusion.g_next
  117.3 8.7 %collective-permute-done.14 = bf16[128,1024]{1,0:T(8,128)(2,1)S(1)} collective-permute-done((bf16[128,1024]{1,0:T(8,128)(2,1)}, bf16[128,1024]{1,0:T(8,128)(2,1)S(1)}, u32[]{:S(2)}, u32[]{:S(2)}) %collective-permute-start.14) | collective-permute-done | bytes 262176 | tf_op jit(solution)/shard_map/ppermute | solution.py:324
  126.2 14.5 %attend1.1 = (bf16[256,1024]{1,0:T(8,128)(2,1)S(1)}, bf16[256,1024]{1,0:T(8,128)(2,1)S(1)}, f32[256,1024]{1,0:T(8,128)S(1)}, f32[256,1024]{1,0:T(8,128)S(1)}, f32[256,128]{1,0:T(8,128)S(1)}) custom-call(s32[9]{0:T(128)S(1)} %pad_add_fusion.1.info, bf16[512,1024]{1,0:T(8,128)(2,1)S(1)} %copy-done.26, bf16[512,1024]{1,0:T(8,128)(2,1)S(1)} %get-tuple-element.46.k, ...), custom_call_target="tpu_custom_call" | custom-call | flops 3221225472 | bytes 6291456 | tf_op jit(solution)/shard_map/attend1/pallas_call | solution.py:85
  140.7 3.3 %weight0.1 = (bf16[16,32,1024]{2,1,0:T(8,128)(2,1)S(1)}, bf16[16,32,1024]{2,1,0:T(8,128)(2,1)S(1)}) custom-call(s32[9]{0:T(128)S(1)} %pad_add_fusion.1.info, bf16[512,1024]{1,0:T(8,128)(2,1)S(1)} %copy-done.24, bf16[512,1024]{1,0:T(8,128)(2,1)S(1)} %copy-done.24, bf16[256,1024]{1,0:T(8,128)(2,1)S(1)} %copy-done.18, bf16[256,1024]{1,0:T(8,128)(2,1)S(1)} %get-tuple-element.64.rb.dq), custom_call_target="tpu_custom_call" | custom-call | flops 1073741824 | bytes 4194304 | tf_op jit(solution)/shard_map/weight0/pallas_call | solution.py:85
  144.2 2.0 collective-permute-start.17
  146.3 3.3 %weight3.1 = (bf16[16,32,1024]{2,1,0:T(8,128)(2,1)S(1)}, bf16[16,32,1024]{2,1,0:T(8,128)(2,1)S(1)}) custom-call(s32[9]{0:T(128)S(1)} %pad_add_fusion.1.info, bf16[256,1024]{1,0:T(8,128)(2,1)S(1)} %copy-done.28, bf16[256,1024]{1,0:T(8,128)(2,1)S(1)} %get-tuple-element.82.lb, bf16[256,1024]{1,0:T(8,128)(2,1)S(1)} %bitcast.78, ...), custom_call_target="tpu_custom_call" | custom-call | flops 1073741824 | bytes 4194304 | tf_op jit(solution)/shard_map/weight3/pallas_call | solution.py:85
  149.6 9.0 %collective-permute-done.17.s_prev = f32[128,128]{1,0:T(8,128)S(1)} collective-permute-done((f32[128,128]{1,0:T(8,128)S(1)}, f32[128,128]{1,0:T(8,128)S(1)}, u32[]{:S(2)}, u32[]{:S(2)}) %collective-permute-start.17) | collective-permute-done | bytes 65568 | tf_op jit(solution)/shard_map/ppermute | solution.py:315
  158.6 11.3 %finish1.1 = (bf16[256,1024]{1,0:T(8,128)(2,1)S(1)}, bf16[256,1024]{1,0:T(8,128)(2,1)S(1)}, bf16[256,1024]{1,0:T(8,128)(2,1)S(1)}) custom-call(s32[9]{0:T(128)S(1)} %pad_add_fusion.1.info, bf16[256,1024]{1,0:T(8,128)(2,1)S(1)} %get-tuple-element.68.qh, bf16[128,1024]{1,0:T(8,128)(2,1)S(1)} %broadcast_select_fusion.1.g_prev, ...), custom_call_target="tpu_custom_call" | custom-call | flops 2684354560 | bytes 13631488 | tf_op jit(solution)/shard_map/finish1/pallas_call | solution.py:85
  170.0 3.3 %weight2.1 = (bf16[16,32,1024]{2,1,0:T(8,128)(2,1)S(1)}, bf16[16,32,1024]{2,1,0:T(8,128)(2,1)S(1)}) custom-call(s32[9]{0:T(128)S(1)} %pad_add_fusion.1.info, bf16[512,1024]{1,0:T(8,128)(2,1)S(1)} %copy-done.24, bf16[512,1024]{1,0:T(8,128)(2,1)S(1)} %copy-done.24, bf16[256,1024]{1,0:T(8,128)(2,1)S(1)} %copy-done.22, bf16[256,1024]{1,0:T(8,128)(2,1)S(1)} %get-tuple-element.78.rb), custom_call_target="tpu_custom_call" | custom-call | flops 1073741824 | bytes 4194304 | tf_op jit(solution)/shard_map/weight2/pallas_call | solution.py:85
  173.3 0.3 collective-permute-start.23
  173.6 3.3 %weight1.1 = (bf16[16,32,1024]{2,1,0:T(8,128)(2,1)S(1)}, bf16[16,32,1024]{2,1,0:T(8,128)(2,1)S(1)}) custom-call(s32[9]{0:T(128)S(1)} %pad_add_fusion.1.info, bf16[512,1024]{1,0:T(8,128)(2,1)S(1)} %copy-done.24, bf16[512,1024]{1,0:T(8,128)(2,1)S(1)} %copy-done.24, bf16[256,1024]{1,0:T(8,128)(2,1)S(1)} %copy-done.20, bf16[256,1024]{1,0:T(8,128)(2,1)S(1)} %get-tuple-element.74.rb), custom_call_target="tpu_custom_call" | custom-call | flops 1073741824 | bytes 4194304 | tf_op jit(solution)/shard_map/weight1/pallas_call | solution.py:85
  177.0 0.4 add_convert_fusion.7
  177.4 2.1 collective-permute-start.10
  179.5 0.4 add_convert_fusion.1
  179.9 3.3 %collective-permute-start.28 = (bf16[8,32,1024]{2,1,0:T(8,128)(2,1)S(1)}, bf16[8,32,1024]{2,1,0:T(8,128)(2,1)S(1)}, u32[]{:S(2)}, u32[]{:S(2)}) collective-permute-start(bf16[8,32,1024]{2,1,0:T(8,128)(2,1)S(1)} %get-tuple-element.99), channel_id=1, source_target_pairs={{0,24},{1,25},{2,26},{3,27},{4,28},{5,29},{6,30},{7,31},{8,16},{9,... | collective-permute-start | bytes 1572872 | tf_op jit(solution)/shard_map/ppermute | solution.py:307
  183.2 16.4 %collective-permute-done.23 = bf16[16,32,1024]{2,1,0:T(8,128)(2,1)S(1)} collective-permute-done((bf16[16,32,1024]{2,1,0:T(8,128)(2,1)S(1)}, bf16[16,32,1024]{2,1,0:T(8,128)(2,1)S(1)}, u32[]{:S(2)}, u32[]{:S(2)}) %collective-permute-start.23) | collective-permute-done | bytes 1048608 | tf_op jit(solution)/shard_map/ppermute | solution.py:307
  199.6 0.4 add_convert_fusion.3
  200.1 4.1 %collective-permute-done.19 = bf16[16,32,1024]{2,1,0:T(8,128)(2,1)S(1)} collective-permute-done((bf16[16,32,1024]{2,1,0:T(8,128)(2,1)S(1)}, bf16[16,32,1024]{2,1,0:T(8,128)(2,1)S(1)}, u32[]{:S(2)}, u32[]{:S(2)}) %collective-permute-start.19) | collective-permute-done | bytes 1048608 | tf_op jit(solution)/shard_map/ppermute | solution.py:307
  204.2 0.4 add_convert_fusion.5
  204.7 5.2 %collective-permute-done.10 = bf16[8,32,1024]{2,1,0:T(8,128)(2,1)S(1)} collective-permute-done((bf16[8,32,1024]{2,1,0:T(8,128)(2,1)S(1)}, bf16[8,32,1024]{2,1,0:T(8,128)(2,1)S(1)}, u32[]{:S(2)}, u32[]{:S(2)}) %collective-permute-start.10) | collective-permute-done | bytes 524320 | tf_op jit(solution)/shard_map/ppermute | solution.py:307
  210.2 5.2 %collective-permute-done.28 = bf16[8,32,1024]{2,1,0:T(8,128)(2,1)S(1)} collective-permute-done((bf16[8,32,1024]{2,1,0:T(8,128)(2,1)S(1)}, bf16[8,32,1024]{2,1,0:T(8,128)(2,1)S(1)}, u32[]{:S(2)}, u32[]{:S(2)}) %collective-permute-start.28) | collective-permute-done | bytes 524320 | tf_op jit(solution)/shard_map/ppermute | solution.py:307
  215.6 2.1 collective-permute-start.29
  217.7 0.2 add_convert_fusion.11
  218.1 0.2 add_convert_fusion.13
  218.4 1.8 collective-permute-done.11
  220.2 1.5 collective-permute-start.12
  221.7 0.5 collective-permute-done.29
  222.3 1.6 collective-permute-start.30
  223.9 3.1 %collective-permute-done.25 = bf16[4,32,1024]{2,1,0:T(8,128)(2,1)S(1)} collective-permute-done((bf16[4,32,1024]{2,1,0:T(8,128)(2,1)S(1)}, bf16[4,32,1024]{2,1,0:T(8,128)(2,1)S(1)}, u32[]{:S(2)}, u32[]{:S(2)}) %collective-permute-start.25) | collective-permute-done | bytes 262176 | tf_op jit(solution)/shard_map/ppermute | solution.py:307
  227.4 1.0 collective-permute-done.12
  228.5 4.8 %collective-permute-done.26 = bf16[2,32,1024]{2,1,0:T(8,128)(2,1)S(1)} collective-permute-done((bf16[2,32,1024]{2,1,0:T(8,128)(2,1)S(1)}, bf16[2,32,1024]{2,1,0:T(8,128)(2,1)S(1)}, u32[]{:S(2)}, u32[]{:S(2)}) %collective-permute-start.26) | collective-permute-done | bytes 131104 | tf_op jit(solution)/shard_map/ppermute | solution.py:307
  233.5 0.3 collective-permute-start.31
  233.8 1.1 maximum_bitcast_fusion
  234.9 11.8 %collective-permute-done.31 = bf16[32,4,1024]{2,0,1:T(8,128)(2,1)S(1)} collective-permute-done((bf16[32,4,1024]{2,0,1:T(8,128)(2,1)S(1)}, bf16[32,4,1024]{2,0,1:T(8,128)(2,1)S(1)}, u32[]{:S(2)}, u32[]{:S(2)}) %collective-permute-start.31) | collective-permute-done | bytes 262176 | tf_op jit(solution)/shard_map/ppermute | solution.py:307
  246.7 1.1 copy.16
  (117 shorter events, 3.0 us)
Async XLA Ops:
  0.6 18.6 %copy-start = (s32[64]{0:T(128)S(1)}, s32[64]{0:T(128)}, u32[]{:S(2)}) copy-start(s32[64]{0:T(128)} %param.18) | copy-start | bytes 772
  0.6 18.8 %copy-start.31 = (s32[2,2]{1,0:T(2,128)S(1)}, s32[2,2]{1,0:T(2,128)}, u32[]{:S(2)}) copy-start(s32[2,2]{1,0:T(2,128)} %param.17) | copy-start | bytes 52
  0.7 19.9 %copy-start.1 = (bf16[1,1024,1024]{2,1,0:T(8,128)(2,1)S(1)}, bf16[1,1024,1024]{2,1,0:T(8,128)(2,1)}, u32[]{:S(2)}) copy-start(bf16[1,1024,1024]{2,1,0:T(8,128)(2,1)} %param.11) | copy-start | bytes 6291460
  8.3 23.9 %collective-permute-start.1 = (bf16[128,1024]{1,0:T(8,128)(2,1)}, bf16[128,1024]{1,0:T(8,128)(2,1)S(1)}, u32[]{:S(2)}, u32[]{:S(2)}) collective-permute-start(bf16[128,1024]{1,0:T(8,128)(2,1)} %get-tuple-element.101), channel_id=1, source_target_pairs={{0,31},{1,0},{2,1},{3,2},{4,3},{5,4},{6,5},{7,6},{8,7},{9,8},{10,9... | collective-permute-start | bytes 786440 | tf_op jit(solution)/shard_map/ppermute | solution.py:315
  19.2 21.9 %collective-permute-start = (bf16[128,1024]{1,0:T(8,128)(2,1)}, bf16[128,1024]{1,0:T(8,128)(2,1)}, u32[]{:S(2)}, u32[]{:S(2)}) collective-permute-start(bf16[128,1024]{1,0:T(8,128)(2,1)} %get-tuple-element.102), channel_id=1, source_target_pairs={{0,1},{1,2},{2,3},{3,4},{4,5},{5,6},{6,7},{7,8},{8,9},{9,10},{10,1... | collective-permute-start | bytes 786440 | tf_op jit(solution)/shard_map/ppermute | solution.py:315
  20.5 1.6 copy-start.2
  22.1 1.6 copy-start.4
  23.7 1.4 copy-start.6
  25.1 6.0 %copy-start.13 = (bf16[1,256,1024]{2,1,0:T(8,128)(2,1)S(1)}, bf16[1,256,1024]{2,1,0:T(8,128)(2,1)}, u32[]{:S(2)}) copy-start(bf16[1,256,1024]{2,1,0:T(8,128)(2,1)} %param.15) | copy-start | bytes 1572868
  25.1 6.1 %copy-start.29 = (bf16[1,256,1024]{2,1,0:T(8,128)(2,1)S(1)}, bf16[1,256,1024]{2,1,0:T(8,128)(2,1)}, u32[]{:S(2)}) copy-start(bf16[1,256,1024]{2,1,0:T(8,128)(2,1)} %param.16) | copy-start | bytes 1572868
  31.2 9.9 %copy-start.23 = (bf16[512,1024]{1,0:T(8,128)(2,1)}, bf16[512,1024]{1,0:T(8,128)(2,1)S(1)}, u32[]{:S(2)}) copy-start(bf16[512,1024]{1,0:T(8,128)(2,1)S(1)} %get-tuple-element.44.la.lb) | copy-start | bytes 3145732
  31.2 25.4 %copy-start.25 = (bf16[512,1024]{1,0:T(8,128)(2,1)}, bf16[512,1024]{1,0:T(8,128)(2,1)S(1)}, u32[]{:S(2)}) copy-start(bf16[512,1024]{1,0:T(8,128)(2,1)S(1)} %get-tuple-element.45.q) | copy-start | bytes 3145732
  31.2 54.6 %copy-start.11 = (bf16[512,1024]{1,0:T(8,128)(2,1)}, bf16[512,1024]{1,0:T(8,128)(2,1)S(1)}, u32[]{:S(2)}) copy-start(bf16[512,1024]{1,0:T(8,128)(2,1)S(1)} %get-tuple-element.47.v) | copy-start | bytes 3145732
  41.1 15.5 %copy-start.9 = (bf16[1,1024,1024]{2,1,0:T(8,128)(2,1)S(1)}, bf16[1,1024,1024]{2,1,0:T(8,128)(2,1)}, u32[]{:S(2)}) copy-start(bf16[1,1024,1024]{2,1,0:T(8,128)(2,1)} %param.14) | copy-start | bytes 6291460
  41.1 44.7 %collective-permute-start.4 = (bf16[128,1024]{1,0:T(8,128)(2,1)S(1)}, bf16[128,1024]{1,0:T(8,128)(2,1)S(1)}, u32[]{:S(2)}, u32[]{:S(2)}) collective-permute-start(bf16[128,1024]{1,0:T(8,128)(2,1)S(1)} %get-tuple-element.58), channel_id=1, source_target_pairs={{0,1},{1,2},{2,3},{3,4},{4,5},{5,6},{6,7},{7,8},{8,9},{9,10},{10,1... | collective-permute-start | bytes 786440 | tf_op jit(solution)/shard_map/ppermute | solution.py:315
  41.2 44.7 %collective-permute-start.5 = (bf16[128,1024]{1,0:T(8,128)(2,1)S(1)}, bf16[128,1024]{1,0:T(8,128)(2,1)S(1)}, u32[]{:S(2)}, u32[]{:S(2)}) collective-permute-start(bf16[128,1024]{1,0:T(8,128)(2,1)S(1)} %get-tuple-element.59), channel_id=1, source_target_pairs={{0,31},{1,0},{2,1},{3,2},{4,3},{5,4},{6,5},{7,6},{8,7},{9,8},{10,9... | collective-permute-start | bytes 786440 | tf_op jit(solution)/shard_map/ppermute | solution.py:315
  56.6 29.2 %copy-start.7 = (bf16[1,3,256,1024]{3,2,1,0:T(8,128)(2,1)S(1)}, bf16[1,3,256,1024]{3,2,1,0:T(8,128)(2,1)}, u32[]{:S(2)}) copy-start(bf16[1,3,256,1024]{3,2,1,0:T(8,128)(2,1)} %param.10) | copy-start | bytes 4718596
  71.2 26.1 %copy-start.17 = (bf16[256,1024]{1,0:T(8,128)(2,1)}, bf16[256,1024]{1,0:T(8,128)(2,1)S(1)}, u32[]{:S(2)}) copy-start(bf16[256,1024]{1,0:T(8,128)(2,1)S(1)} %get-tuple-element.52.dq.ra) | copy-start | bytes 1572868
  71.2 26.1 %copy-start.27 = (bf16[256,1024]{1,0:T(8,128)(2,1)}, bf16[256,1024]{1,0:T(8,128)(2,1)S(1)}, u32[]{:S(2)}) copy-start(bf16[256,1024]{1,0:T(8,128)(2,1)S(1)} %get-tuple-element.81.la) | copy-start | bytes 1572868
  71.2 4.3 %collective-permute-start.7 = (f32[128,128]{1,0:T(8,128)S(1)}, f32[128,128]{1,0:T(8,128)S(1)}, u32[]{:S(2)}, u32[]{:S(2)}) collective-permute-start(f32[128,128]{1,0:T(8,128)S(1)} %get-tuple-element.136), channel_id=1, source_target_pairs={{0,31},{1,0},{2,1},{3,2},{4,3},{5,4},{6,5},{7,6},{8,7},{9,8},{10,9... | collective-permute-start | bytes 196616 | tf_op jit(solution)/shard_map/ppermute | solution.py:315
  71.3 13.2 %collective-permute-start.6 = (f32[128,128]{1,0:T(8,128)S(1)}, f32[128,128]{1,0:T(8,128)S(1)}, u32[]{:S(2)}, u32[]{:S(2)}) collective-permute-start(f32[128,128]{1,0:T(8,128)S(1)} %get-tuple-element.137), channel_id=1, source_target_pairs={{0,1},{1,2},{2,3},{3,4},{4,5},{5,6},{6,7},{7,8},{8,9},{9,10},{10,1... | collective-permute-start | bytes 196616 | tf_op jit(solution)/shard_map/ppermute | solution.py:315
  73.3 28.2 %collective-permute-start.2 = (bf16[128,1024]{1,0:T(8,128)(2,1)}, bf16[128,1024]{1,0:T(8,128)(2,1)S(1)}, u32[]{:S(2)}, u32[]{:S(2)}) collective-permute-start(bf16[128,1024]{1,0:T(8,128)(2,1)} %get-tuple-element.53), channel_id=1, source_target_pairs={{0,1},{1,2},{2,3},{3,4},{4,5},{5,6},{6,7},{7,8},{8,9},{9,10},{10,1... | collective-permute-start | bytes 786440 | tf_op jit(solution)/shard_map/ppermute | solution.py:315
  75.5 28.5 %collective-permute-start.3 = (bf16[128,1024]{1,0:T(8,128)(2,1)}, bf16[128,1024]{1,0:T(8,128)(2,1)}, u32[]{:S(2)}, u32[]{:S(2)}) collective-permute-start(bf16[128,1024]{1,0:T(8,128)(2,1)} %get-tuple-element.54), channel_id=1, source_target_pairs={{0,31},{1,0},{2,1},{3,2},{4,3},{5,4},{6,5},{7,6},{8,7},{9,8},{10,9... | collective-permute-start | bytes 786440 | tf_op jit(solution)/shard_map/ppermute | solution.py:315
  84.5 31.6 %collective-permute-start.15 = (bf16[128,1024]{1,0:T(8,128)(2,1)}, bf16[128,1024]{1,0:T(8,128)(2,1)}, u32[]{:S(2)}, u32[]{:S(2)}) collective-permute-start(bf16[128,1024]{1,0:T(8,128)(2,1)} %get-tuple-element.70), channel_id=1, source_target_pairs={{224,255},{225,224},{226,225},{227,226},{228,227},{229,228},{230,2... | collective-permute-start | bytes 786440 | tf_op jit(solution)/shard_map/ppermute | solution.py:330
  97.2 0.8 copy-start.15
  97.2 1.6 copy-start.19
  97.3 1.6 copy-start.21
  98.9 17.2 %collective-permute-start.16 = (bf16[128,1024]{1,0:T(8,128)(2,1)}, bf16[128,1024]{1,0:T(8,128)(2,1)}, u32[]{:S(2)}, u32[]{:S(2)}) collective-permute-start(bf16[128,1024]{1,0:T(8,128)(2,1)} %get-tuple-element.118), channel_id=1, source_target_pairs={{32,31},{33,0},{34,1},{35,2},{36,3},{37,4},{38,5},{39,6},{40,7},{4... | collective-permute-start | bytes 786440 | tf_op jit(solution)/shard_map/ppermute | solution.py:324
  100.8 16.4 %collective-permute-start.13 = (bf16[128,1024]{1,0:T(8,128)(2,1)}, bf16[128,1024]{1,0:T(8,128)(2,1)S(1)}, u32[]{:S(2)}, u32[]{:S(2)}) collective-permute-start(bf16[128,1024]{1,0:T(8,128)(2,1)} %get-tuple-element.69), channel_id=1, source_target_pairs={{224,225},{225,226},{226,227},{227,228},{228,229},{229,230},{230,2... | collective-permute-start | bytes 786440 | tf_op jit(solution)/shard_map/ppermute | solution.py:330
  101.5 24.5 %collective-permute-start.8 = (bf16[256,1024]{1,0:T(8,128)(2,1)}, bf16[256,1024]{1,0:T(8,128)(2,1)S(1)}, u32[]{:S(2)}, u32[]{:S(2)}) collective-permute-start(bf16[256,1024]{1,0:T(8,128)(2,1)} %copy-done.15), channel_id=1, source_target_pairs={{32,0},{33,1},{34,2},{35,3},{36,4},{37,5},{38,6},{39,7},{40,8},{41... | collective-permute-start | bytes 1572872 | tf_op jit(solution)/shard_map/ppermute | solution.py:324
  104.0 22.0 %collective-permute-start.14 = (bf16[128,1024]{1,0:T(8,128)(2,1)}, bf16[128,1024]{1,0:T(8,128)(2,1)S(1)}, u32[]{:S(2)}, u32[]{:S(2)}) collective-permute-start(bf16[128,1024]{1,0:T(8,128)(2,1)} %get-tuple-element.119), channel_id=1, source_target_pairs={{32,1},{33,2},{34,3},{35,4},{36,5},{37,6},{38,7},{39,8},{40,9},{41... | collective-permute-start | bytes 786440 | tf_op jit(solution)/shard_map/ppermute | solution.py:324
  107.6 1.6 copy-start.3
  109.1 1.6 copy-start.5
  110.7 15.3 %copy-start.30 = (bf16[1,256,1024]{2,1,0:T(8,128)(2,1)S(1)}, bf16[1,256,1024]{2,1,0:T(8,128)(2,1)}, u32[]{:S(2)}) copy-start(bf16[1,256,1024]{2,1,0:T(8,128)(2,1)} %param.16) | copy-start | bytes 1572868
  110.7 15.4 %copy-start.26 = (bf16[512,1024]{1,0:T(8,128)(2,1)S(1)}, bf16[512,1024]{1,0:T(8,128)(2,1)}, u32[]{:S(2)}) copy-start(bf16[512,1024]{1,0:T(8,128)(2,1)} %copy-done.25) | copy-start | bytes 3145732
  116.1 10.0 %copy-start.10 = (bf16[1,1024,1024]{2,1,0:T(8,128)(2,1)S(1)}, bf16[1,1024,1024]{2,1,0:T(8,128)(2,1)}, u32[]{:S(2)}) copy-start(bf16[1,1024,1024]{2,1,0:T(8,128)(2,1)} %param.14) | copy-start | bytes 6291460
  116.1 10.0 %copy-start.12 = (bf16[512,1024]{1,0:T(8,128)(2,1)S(1)}, bf16[512,1024]{1,0:T(8,128)(2,1)}, u32[]{:S(2)}) copy-start(bf16[512,1024]{1,0:T(8,128)(2,1)} %copy-done.11) | copy-start | bytes 3145732
  126.2 14.5 %copy-start.18 = (bf16[256,1024]{1,0:T(8,128)(2,1)S(1)}, bf16[256,1024]{1,0:T(8,128)(2,1)}, u32[]{:S(2)}) copy-start(bf16[256,1024]{1,0:T(8,128)(2,1)} %copy-done.17) | copy-start | bytes 1572868
  126.2 14.5 %copy-start.24 = (bf16[512,1024]{1,0:T(8,128)(2,1)S(1)}, bf16[512,1024]{1,0:T(8,128)(2,1)}, u32[]{:S(2)}) copy-start(bf16[512,1024]{1,0:T(8,128)(2,1)} %copy-done.23) | copy-start | bytes 3145732
  140.7 5.5 %copy-start.14 = (bf16[1,256,1024]{2,1,0:T(8,128)(2,1)S(1)}, bf16[1,256,1024]{2,1,0:T(8,128)(2,1)}, u32[]{:S(2)}) copy-start(bf16[1,256,1024]{2,1,0:T(8,128)(2,1)} %param.15) | copy-start | bytes 1572868
  140.7 5.5 %copy-start.28 = (bf16[256,1024]{1,0:T(8,128)(2,1)S(1)}, bf16[256,1024]{1,0:T(8,128)(2,1)}, u32[]{:S(2)}) copy-start(bf16[256,1024]{1,0:T(8,128)(2,1)} %copy-done.27) | copy-start | bytes 1572868
  144.0 33.0 %collective-permute-start.9 = (bf16[16,32,1024]{2,1,0:T(8,128)(2,1)S(1)}, bf16[16,32,1024]{2,1,0:T(8,128)(2,1)S(1)}, u32[]{:S(2)}, u32[]{:S(2)}) collective-permute-start(bf16[16,32,1024]{2,1,0:T(8,128)(2,1)S(1)} %get-tuple-element.66), channel_id=1, source_target_pairs={{0,8},{1,9},{2,10},{3,11},{4,12},{5,13},{6,14},{7,15},{8,0},{9,1},... | collective-permute-start | bytes 3145736 | tf_op jit(solution)/shard_map/ppermute | solution.py:307
  144.1 14.5 %copy-start.8 = (bf16[1,3,256,1024]{3,2,1,0:T(8,128)(2,1)S(1)}, bf16[1,3,256,1024]{3,2,1,0:T(8,128)(2,1)}, u32[]{:S(2)}) copy-start(bf16[1,3,256,1024]{3,2,1,0:T(8,128)(2,1)} %param.10) | copy-start | bytes 4718596
  144.1 5.5 %collective-permute-start.18 = (f32[128,128]{1,0:T(8,128)S(1)}, f32[128,128]{1,0:T(8,128)S(1)}, u32[]{:S(2)}, u32[]{:S(2)}) collective-permute-start(f32[128,128]{1,0:T(8,128)S(1)} %get-tuple-element.134), channel_id=1, source_target_pairs={{0,31},{1,0},{2,1},{3,2},{4,3},{5,4},{6,5},{7,6},{8,7},{9,8},{10,9... | collective-permute-start | bytes 196616 | tf_op jit(solution)/shard_map/ppermute | solution.py:315
  144.2 14.4 %collective-permute-start.17 = (f32[128,128]{1,0:T(8,128)S(1)}, f32[128,128]{1,0:T(8,128)S(1)}, u32[]{:S(2)}, u32[]{:S(2)}) collective-permute-start(f32[128,128]{1,0:T(8,128)S(1)} %get-tuple-element.135), channel_id=1, source_target_pairs={{0,1},{1,2},{2,3},{3,4},{4,5},{5,6},{6,7},{7,8},{8,9},{9,10},{10,1... | collective-permute-start | bytes 196616 | tf_op jit(solution)/shard_map/ppermute | solution.py:315
  149.5 30.0 %collective-permute-start.27 = (bf16[16,32,1024]{2,1,0:T(8,128)(2,1)S(1)}, bf16[16,32,1024]{2,1,0:T(8,128)(2,1)S(1)}, u32[]{:S(2)}, u32[]{:S(2)}) collective-permute-start(bf16[16,32,1024]{2,1,0:T(8,128)(2,1)S(1)} %get-tuple-element.84), channel_id=1, source_target_pairs={{0,3},{1,2},{2,1},{3,0},{4,7},{5,6},{6,5},{7,4},{8,11},{9,10},{10,... | collective-permute-start | bytes 3145736 | tf_op jit(solution)/shard_map/ppermute | solution.py:307
  158.6 11.3 %copy-start.22 = (bf16[256,1024]{1,0:T(8,128)(2,1)S(1)}, bf16[256,1024]{1,0:T(8,128)(2,1)}, u32[]{:S(2)}) copy-start(bf16[256,1024]{1,0:T(8,128)(2,1)} %copy-done.21) | copy-start | bytes 1572868
  170.0 3.6 %copy-start.20 = (bf16[256,1024]{1,0:T(8,128)(2,1)S(1)}, bf16[256,1024]{1,0:T(8,128)(2,1)}, u32[]{:S(2)}) copy-start(bf16[256,1024]{1,0:T(8,128)(2,1)} %copy-done.19) | copy-start | bytes 1572868
  173.3 26.3 %collective-permute-start.23 = (bf16[16,32,1024]{2,1,0:T(8,128)(2,1)S(1)}, bf16[16,32,1024]{2,1,0:T(8,128)(2,1)S(1)}, u32[]{:S(2)}, u32[]{:S(2)}) collective-permute-start(bf16[16,32,1024]{2,1,0:T(8,128)(2,1)S(1)} %get-tuple-element.80), channel_id=1, source_target_pairs={{0,1},{1,0},{2,3},{3,2},{4,5},{5,4},{6,7},{7,6},{8,9},{9,8},{10,11... | collective-permute-start | bytes 3145736 | tf_op jit(solution)/shard_map/ppermute | solution.py:307
  176.9 27.3 %collective-permute-start.19 = (bf16[16,32,1024]{2,1,0:T(8,128)(2,1)S(1)}, bf16[16,32,1024]{2,1,0:T(8,128)(2,1)S(1)}, u32[]{:S(2)}, u32[]{:S(2)}) collective-permute-start(bf16[16,32,1024]{2,1,0:T(8,128)(2,1)S(1)} %get-tuple-element.76), channel_id=1, source_target_pairs={{0,24},{1,25},{2,26},{3,27},{4,28},{5,29},{6,30},{7,31},{8,16},{9,... | collective-permute-start | bytes 3145736 | tf_op jit(solution)/shard_map/ppermute | solution.py:307
  177.4 32.5 %collective-permute-start.10 = (bf16[8,32,1024]{2,1,0:T(8,128)(2,1)S(1)}, bf16[8,32,1024]{2,1,0:T(8,128)(2,1)S(1)}, u32[]{:S(2)}, u32[]{:S(2)}) collective-permute-start(bf16[8,32,1024]{2,1,0:T(8,128)(2,1)S(1)} %get-tuple-element.93), channel_id=1, source_target_pairs={{0,1},{1,0},{2,3},{3,2},{4,5},{5,4},{6,7},{7,6},{8,9},{9,8},{10,11... | collective-permute-start | bytes 1572872 | tf_op jit(solution)/shard_map/ppermute | solution.py:307
  179.9 35.5 %collective-permute-start.28 = (bf16[8,32,1024]{2,1,0:T(8,128)(2,1)S(1)}, bf16[8,32,1024]{2,1,0:T(8,128)(2,1)S(1)}, u32[]{:S(2)}, u32[]{:S(2)}) collective-permute-start(bf16[8,32,1024]{2,1,0:T(8,128)(2,1)S(1)} %get-tuple-element.99), channel_id=1, source_target_pairs={{0,24},{1,25},{2,26},{3,27},{4,28},{5,29},{6,30},{7,31},{8,16},{9,... | collective-permute-start | bytes 1572872 | tf_op jit(solution)/shard_map/ppermute | solution.py:307
  200.0 17.7 %collective-permute-start.24 = (bf16[8,32,1024]{2,1,0:T(8,128)(2,1)S(1)}, bf16[8,32,1024]{2,1,0:T(8,128)(2,1)S(1)}, u32[]{:S(2)}, u32[]{:S(2)}) collective-permute-start(bf16[8,32,1024]{2,1,0:T(8,128)(2,1)S(1)} %get-tuple-element.97), channel_id=1, source_target_pairs={{0,8},{1,9},{2,10},{3,11},{4,12},{5,13},{6,14},{7,15},{8,0},{9,1},... | collective-permute-start | bytes 1572872 | tf_op jit(solution)/shard_map/ppermute | solution.py:307
  204.6 13.4 %collective-permute-start.20 = (bf16[8,32,1024]{2,1,0:T(8,128)(2,1)S(1)}, bf16[8,32,1024]{2,1,0:T(8,128)(2,1)S(1)}, u32[]{:S(2)}, u32[]{:S(2)}) collective-permute-start(bf16[8,32,1024]{2,1,0:T(8,128)(2,1)S(1)} %get-tuple-element.95), channel_id=1, source_target_pairs={{0,3},{1,2},{2,1},{3,0},{4,7},{5,6},{6,5},{7,4},{8,11},{9,10},{10,... | collective-permute-start | bytes 1572872 | tf_op jit(solution)/shard_map/ppermute | solution.py:307
  210.1 10.0 %collective-permute-start.11 = (bf16[4,32,1024]{2,1,0:T(8,128)(2,1)S(1)}, bf16[4,32,1024]{2,1,0:T(8,128)(2,1)S(1)}, u32[]{:S(2)}, u32[]{:S(2)}) collective-permute-start(bf16[4,32,1024]{2,1,0:T(8,128)(2,1)S(1)} %get-tuple-element.105), channel_id=1, source_target_pairs={{0,24},{1,25},{2,26},{3,27},{4,28},{5,29},{6,30},{7,31},{8,16},{9,... | collective-permute-start | bytes 786440 | tf_op jit(solution)/shard_map/ppermute | solution.py:307
  215.6 6.6 %collective-permute-start.29 = (bf16[4,32,1024]{2,1,0:T(8,128)(2,1)S(1)}, bf16[4,32,1024]{2,1,0:T(8,128)(2,1)S(1)}, u32[]{:S(2)}, u32[]{:S(2)}) collective-permute-start(bf16[4,32,1024]{2,1,0:T(8,128)(2,1)S(1)} %get-tuple-element.111), channel_id=1, source_target_pairs={{0,1},{1,0},{2,3},{3,2},{4,5},{5,4},{6,7},{7,6},{8,9},{9,8},{10,11... | collective-permute-start | bytes 786440 | tf_op jit(solution)/shard_map/ppermute | solution.py:307
  217.9 9.1 %collective-permute-start.25 = (bf16[4,32,1024]{2,1,0:T(8,128)(2,1)S(1)}, bf16[4,32,1024]{2,1,0:T(8,128)(2,1)S(1)}, u32[]{:S(2)}, u32[]{:S(2)}) collective-permute-start(bf16[4,32,1024]{2,1,0:T(8,128)(2,1)S(1)} %get-tuple-element.109), channel_id=1, source_target_pairs={{0,3},{1,2},{2,1},{3,0},{4,7},{5,6},{6,5},{7,4},{8,11},{9,10},{10,... | collective-permute-start | bytes 786440 | tf_op jit(solution)/shard_map/ppermute | solution.py:307
  218.3 8.9 %collective-permute-start.21 = (bf16[4,32,1024]{2,1,0:T(8,128)(2,1)S(1)}, bf16[4,32,1024]{2,1,0:T(8,128)(2,1)S(1)}, u32[]{:S(2)}, u32[]{:S(2)}) collective-permute-start(bf16[4,32,1024]{2,1,0:T(8,128)(2,1)S(1)} %get-tuple-element.107), channel_id=1, source_target_pairs={{0,8},{1,9},{2,10},{3,11},{4,12},{5,13},{6,14},{7,15},{8,0},{9,1},... | collective-permute-start | bytes 786440 | tf_op jit(solution)/shard_map/ppermute | solution.py:307
  220.2 8.2 %collective-permute-start.12 = (bf16[2,32,1024]{2,1,0:T(8,128)(2,1)S(1)}, bf16[2,32,1024]{2,1,0:T(8,128)(2,1)S(1)}, u32[]{:S(2)}, u32[]{:S(2)}) collective-permute-start(bf16[2,32,1024]{2,1,0:T(8,128)(2,1)S(1)} %get-tuple-element.113), channel_id=1, source_target_pairs={{0,3},{1,2},{2,1},{3,0},{4,7},{5,6},{6,5},{7,4},{8,11},{9,10},{10,... | collective-permute-start | bytes 393224 | tf_op jit(solution)/shard_map/ppermute | solution.py:307
  222.2 11.6 %copy-start.16 = (bf16[256,1024]{1,0:T(8,128)(2,1)S(1)}, bf16[256,1024]{1,0:T(8,128)(2,1)}, u32[]{:S(2)}) copy-start(bf16[256,1024]{1,0:T(8,128)(2,1)} %copy-done.15) | copy-start | bytes 1572868
  222.3 6.2 %collective-permute-start.30 = (bf16[2,32,1024]{2,1,0:T(8,128)(2,1)S(1)}, bf16[2,32,1024]{2,1,0:T(8,128)(2,1)S(1)}, u32[]{:S(2)}, u32[]{:S(2)}) collective-permute-start(bf16[2,32,1024]{2,1,0:T(8,128)(2,1)S(1)} %get-tuple-element.121), channel_id=1, source_target_pairs={{0,8},{1,9},{2,10},{3,11},{4,12},{5,13},{6,14},{7,15},{8,0},{9,1},... | collective-permute-start | bytes 393224 | tf_op jit(solution)/shard_map/ppermute | solution.py:307
  227.1 6.3 %collective-permute-start.26 = (bf16[2,32,1024]{2,1,0:T(8,128)(2,1)S(1)}, bf16[2,32,1024]{2,1,0:T(8,128)(2,1)S(1)}, u32[]{:S(2)}, u32[]{:S(2)}) collective-permute-start(bf16[2,32,1024]{2,1,0:T(8,128)(2,1)S(1)} %get-tuple-element.117), channel_id=1, source_target_pairs={{0,24},{1,25},{2,26},{3,27},{4,28},{5,29},{6,30},{7,31},{8,16},{9,... | collective-permute-start | bytes 393224 | tf_op jit(solution)/shard_map/ppermute | solution.py:307
  227.3 6.1 %collective-permute-start.22 = (bf16[2,32,1024]{2,1,0:T(8,128)(2,1)S(1)}, bf16[2,32,1024]{2,1,0:T(8,128)(2,1)S(1)}, u32[]{:S(2)}, u32[]{:S(2)}) collective-permute-start(bf16[2,32,1024]{2,1,0:T(8,128)(2,1)S(1)} %get-tuple-element.115), channel_id=1, source_target_pairs={{0,1},{1,0},{2,3},{3,2},{4,5},{5,4},{6,7},{7,6},{8,9},{9,8},{10,11... | collective-permute-start | bytes 393224 | tf_op jit(solution)/shard_map/ppermute | solution.py:307
  233.5 13.2 %collective-permute-start.31 = (bf16[32,4,1024]{2,0,1:T(8,128)(2,1)S(1)}, bf16[32,4,1024]{2,0,1:T(8,128)(2,1)S(1)}, u32[]{:S(2)}, u32[]{:S(2)}) collective-permute-start(bf16[32,4,1024]{2,0,1:T(8,128)(2,1)S(1)} %pad_maximum_fusion), channel_id=1, source_target_pairs={{0,4},{1,5},{2,6},{3,7},{4,0},{5,1},{6,2},{7,3},{8,12},{9,13},{10,... | collective-permute-start | bytes 786440 | tf_op jit(solution)/shard_map/ppermute | solution.py:307
